TPU v7x, 512 devices: a whole 4x4x16 slice. The times are simulated.
512 devices in a mesh: dp: 4 (over z_lo), tm: 16 (over y, z_hi), patch: 8 (over x, core).
Axes of the slice: x: 4, y: 4, z: 16 (z_hi: 4, z_lo: 4; z = z_hi * 4 + z_lo), core: 2. Of those that a mesh axis runs over, the one named last changes fastest.
Arguments:
- tokens: bfloat16 [1024, 64, 1024], P(('dp', 'tm'), 'patch'), parts along dimension 0, may hold values from -6 to 6
- frame_gain: float32 [1024], replicated, may hold values from 0.5 to 4.5
- qkv_weight: bfloat16 [1024, 3072], P(None, 'tm'), may hold values from -0.1875 to 0.1875
- out_weight: bfloat16 [1024, 1024], P('tm'), may hold values from -0.1875 to 0.1875
- pool_gain: float32 [1024], replicated, may hold values from 0.5 to 4.5
- latent_gain: float32 [1024], replicated, may hold values from 0.5 to 4.5
- latents: bfloat16 [64, 1024], replicated, may hold values from -6 to 6
- query_weight: bfloat16 [1024, 1024], P(None, 'tm'), may hold values from -0.1875 to 0.1875
- kv_weight: bfloat16 [1024, 2048], P(None, 'tm'), may hold values from -0.1875 to 0.1875
- clip_starts: int32 [128], P(('dp', 'tm')), parts along dimension 0, may hold values from -7 to 248, as said below
- valid_frames: int32 [4], P('dp'), parts along dimension 0, may hold values from 128 to 256
Outputs:
- temporal_out: bfloat16 [1024, 64, 1024], P(('dp', 'tm'), 'patch'), parts along dimension 0
- pooled_latents: bfloat16 [128, 64, 1024], P(('dp', 'tm')), parts along dimension 0
There are 4 independent parts, one for each index of `dp`. A program takes and returns all parts, laid end to end along the dimension named above; an argument that names none is the same for every part. Nothing has to cross between parts.
Inputs may be any that keep to these rules, and one draw needn't show every extreme that they name: `clip_starts`: clip c starts at frame 8 * c - k with k from 0 to 7; the first clip has k = 7 and the last k = 0.
All inputs are finite; a program needn't handle non-finite values.
Results may differ from a plain program's by a relative error of at most 0.03.
The roundings to bfloat16 on the way count: a program that leaves them out, or rounds other values in their place, can miss the bound.
Values may be sent and summed in bfloat16 or wider, within the bound.
A program may use at most 64 MiB of HBM per device.

v0:
```python
import jax
import jax.numpy as jnp
from jax import lax
from jax.sharding import PartitionSpec as P

HEADS = 16
LATENTS = 64
CLIP = 16
STRIDE = 8


EPS = 1e-05
NEG = -1e30


def with_halo(block, sides, width):
    for axis, dim in sides:
        count = lax.axis_size(axis)
        forward = [(i, i + 1) for i in range(count - 1)]
        backward = [(target, source) for source, target in forward]
        low = lax.ppermute(
            lax.slice_in_dim(block, block.shape[dim] - width, None, axis=dim), axis, forward
        )
        high = lax.ppermute(lax.slice_in_dim(block, 0, width, axis=dim), axis, backward)
        block = jnp.concatenate([low, block, high], axis=dim)
    return block


def layer_norm(value, gain):
    value = value.astype(jnp.float32)
    center = value - jnp.mean(value, axis=-1, keepdims=True)
    spread = jnp.mean(center * center, axis=-1, keepdims=True)
    return center * lax.rsqrt(spread + EPS) * gain


def on_device(
    tokens,
    frame_gain,
    qkv_weight,
    out_weight,
    pool_gain,
    latent_gain,
    latents,
    query_weight,
    kv_weight,
    clip_starts,
    valid_frames,
):
    frames_dev, patch_dev, width = tokens.shape
    groups = lax.axis_size("tm")
    heads_dev = HEADS // groups
    head_size = width // HEADS
    total_frames = frames_dev * groups
    score_scale = head_size ** (-0.5)
    valid = valid_frames[0]
    normed = layer_norm(tokens, frame_gain).astype(jnp.bfloat16)
    flat_normed = normed.reshape(frames_dev * patch_dev, width)
    projected = jnp.dot(
        flat_normed,
        lax.all_gather(qkv_weight, "tm", axis=1, tiled=True),
        preferred_element_type=jnp.float32,
    ).astype(jnp.bfloat16)
    projected = projected.reshape(frames_dev, patch_dev, 3 * width)
    by_head = lax.all_to_all(projected, "tm", split_axis=2, concat_axis=0, tiled=True)
    by_head = by_head.reshape(total_frames, patch_dev, heads_dev, 3, head_size)
    query_part = by_head[:, :, :, 0]
    key_part = by_head[:, :, :, 1]
    value_part = by_head[:, :, :, 2]
    scores = (
        jnp.einsum("fphe,gphe->phfg", query_part, key_part, preferred_element_type=jnp.float32)
        * score_scale
    )
    key_live = (jnp.arange(total_frames, dtype=jnp.int32) < valid)[None, None, None, :]
    max_score = jnp.max(jnp.where(key_live, scores, -jnp.inf), axis=-1, keepdims=True)
    weights = jnp.where(key_live, jnp.exp(scores - max_score), 0.0)
    weight_total = jnp.sum(weights, axis=-1)
    head_mixed = jnp.einsum(
        "phfg,gphe->fphe",
        weights.astype(jnp.bfloat16),
        value_part,
        preferred_element_type=jnp.float32,
    )
    head_mixed = head_mixed / jnp.transpose(weight_total, (2, 0, 1))[..., None]
    attended = head_mixed.astype(jnp.bfloat16).reshape(
        total_frames, patch_dev, heads_dev * head_size
    )
    frame_heads = lax.all_to_all(attended, "tm", split_axis=0, concat_axis=2, tiled=True)
    flat_heads = frame_heads.reshape(frames_dev * patch_dev, width)
    summed = tokens.reshape(frames_dev * patch_dev, width).astype(jnp.float32) + jnp.dot(
        flat_heads,
        lax.all_gather(out_weight, "tm", axis=0, tiled=True),
        preferred_element_type=jnp.float32,
    )
    temporal_out = summed.astype(jnp.bfloat16).reshape(frames_dev, patch_dev, width)
    pooled = layer_norm(temporal_out, pool_gain).astype(jnp.bfloat16)
    latent_normed = layer_norm(latents, latent_gain).astype(jnp.bfloat16)
    query_shard = jnp.dot(latent_normed, query_weight, preferred_element_type=jnp.float32).astype(
        jnp.bfloat16
    )
    latent_queries = lax.all_gather(query_shard, "tm", axis=1, tiled=True).reshape(
        LATENTS, HEADS, head_size
    )
    extended = with_halo(pooled, (("tm", 0),), STRIDE)
    extended_rows = extended.shape[0] * patch_dev
    source_rows = jnp.concatenate([extended.reshape(extended_rows, width), latent_normed], axis=0)
    pair_rows = jnp.dot(
        source_rows,
        lax.all_gather(kv_weight, "tm", axis=1, tiled=True),
        preferred_element_type=jnp.float32,
    ).astype(jnp.bfloat16)
    clip_kv = pair_rows[:extended_rows].reshape(extended.shape[0], patch_dev, 2 * width)
    latent_kv = pair_rows[extended_rows:]
    clip_kv = clip_kv.reshape(frames_dev + 2 * STRIDE, patch_dev, HEADS, 2, head_size)
    latent_kv = latent_kv.reshape(LATENTS, HEADS, 2, head_size)
    first_frame = lax.axis_index("tm") * frames_dev - STRIDE
    clips_dev = frames_dev // STRIDE
    clip_maxima = []
    clip_totals = []
    clip_mixes = []
    for clip_number in range(clips_dev):
        start = clip_starts[clip_number]
        window = lax.dynamic_slice_in_dim(clip_kv, start - first_frame, CLIP, 0)
        frame_index = start + jnp.arange(CLIP, dtype=jnp.int32)
        live_mask = ((frame_index >= 0) & (frame_index < valid))[None, None, :, None]
        clip_scores = (
            jnp.einsum(
                "lhe,fphe->hlfp",
                latent_queries,
                window[:, :, :, 0],
                preferred_element_type=jnp.float32,
            )
            * score_scale
        )
        clip_max = jnp.max(jnp.where(live_mask, clip_scores, NEG), axis=(2, 3))
        clip_weights = jnp.where(live_mask, jnp.exp(clip_scores - clip_max[:, :, None, None]), 0.0)
        clip_maxima.append(clip_max)
        clip_totals.append(jnp.sum(clip_weights, axis=(2, 3)))
        clip_mixes.append(
            jnp.einsum(
                "hlfp,fphe->hle",
                clip_weights.astype(jnp.bfloat16),
                window[:, :, :, 1],
                preferred_element_type=jnp.float32,
            )
        )
    maxima = jnp.stack(clip_maxima)
    totals = jnp.stack(clip_totals)
    mixes = jnp.stack(clip_mixes)
    highest = lax.pmax(maxima, "patch")
    factor = jnp.exp(maxima - highest)
    totals, mixes = lax.psum((totals * factor, mixes * factor[..., None]), "patch")
    maxima = highest
    self_scores = (
        jnp.einsum(
            "lhe,mhe->hlm", latent_queries, latent_kv[:, :, 0], preferred_element_type=jnp.float32
        )
        * score_scale
    )
    highest = jnp.maximum(maxima, jnp.max(self_scores, axis=-1)[None])
    factor = jnp.exp(maxima - highest)
    self_weights = jnp.exp(self_scores[None] - highest[..., None])
    weight_total = totals * factor + jnp.sum(self_weights, axis=-1)
    combined = mixes * factor[..., None] + jnp.einsum(
        "chlm,mhe->chle",
        self_weights.astype(jnp.bfloat16),
        latent_kv[:, :, 1],
        preferred_element_type=jnp.float32,
    )
    result = combined / weight_total[..., None]
    pooled_latents = (
        jnp.transpose(result, (0, 2, 1, 3)).reshape(clips_dev, LATENTS, width).astype(jnp.bfloat16)
    )
    return (temporal_out, pooled_latents)


def solution(mesh):
    in_specs = (
        P(("dp", "tm"), "patch", None),
        P(),
        P(None, "tm"),
        P("tm", None),
        P(),
        P(),
        P(),
        P(None, "tm"),
        P(None, "tm"),
        P(("dp", "tm")),
        P("dp"),
    )
    out_specs = (P(("dp", "tm"), "patch", None), P(("dp", "tm"), None, None))
    return jax.shard_map(
        on_device, mesh=mesh, in_specs=in_specs, out_specs=out_specs, check_vma=False
    )
```

profile of v0, /device:TPU:8, one launch (start us, length us, event | category | flops | bytes accessed | tf_op | source)
XLA Modules:
  0.0 606.3 jit_solution(16599494739531929996)
XLA Ops:
  11.7 193.2 %all-gather.4.cloned.1.call-done = bf16[1024,3072]{0,1:T(8,128)(2,1)} async-done(((bf16[1024,192]{0,1:T(8,128)(2,1)}), bf16[1024,3072]{0,1:T(8,128)(2,1)}) %all-gather.4.cloned.1.call-update) | async-done | bytes 6291472 | tf_op jit(solution)/shard_map/all_gather | solution.py:60
  204.8 5.1 fusion.1
  209.9 5.6 copy.96
  215.6 9.6 %reshape.171 = bf16[16,2,12288]{2,1,0:T(2,128)(2,1)} reshape(bf16[3072,8,16]{2,1,0:T(8,128)(2,1)} %bitcast.125) | data formatting | bytes 1572864
  225.2 10.2 %all-to-all-start = ((bf16[16,2,12288]{2,1,0:T(2,128)(2,1)}), bf16[16,2,12288]{2,1,0:T(2,128)(2,1)S(1)}, u32[]{:S(2)}, u32[]{:S(2)}) async-start(bf16[16,2,12288]{2,1,0:T(2,128)(2,1)} %reshape.171), calls=%async_computation | async-start | bytes 1572864 | tf_op jit(solution)/shard_map/all_to_all | solution.py:64
  236.3 26.1 %all-to-all-done = bf16[16,2,12288]{2,1,0:T(2,128)(2,1)S(1)} async-done(((bf16[16,2,12288]{2,1,0:T(2,128)(2,1)}), bf16[16,2,12288]{2,1,0:T(2,128)(2,1)S(1)}, u32[]{:S(2)}, u32[]{:S(2)}) %all-to-all-start) | async-done | bytes 786464 | tf_op jit(solution)/shard_map/all_to_all | solution.py:64
  262.4 5.6 reshape.172
  268.0 7.7 %copy.98 = bf16[16,16,8,192]{3,2,1,0:T(8,128)(2,1)S(1)} copy(bf16[16,16,8,192]{1,2,3,0:T(8,128)(2,1)} %bitcast.126) | data formatting | bytes 1572864 | tf_op jit(solution)/shard_map/all_to_all | solution.py:64
  276.4 3.2 fusion.65
  279.6 2.3 copy.134
  281.9 2.3 copy.135
  288.0 10.1 %all-to-all-start.1 = ((bf16[16,2,4096]{2,1,0:T(2,128)(2,1)}), bf16[16,2,4096]{2,1,0:T(2,128)(2,1)S(1)}, u32[]{:S(2)}, u32[]{:S(2)}) async-start(bf16[16,2,4096]{2,1,0:T(2,128)(2,1)} %reshape.173), calls=%async_computation.1 | async-start | bytes 524288 | tf_op jit(solution)/shard_map/all_to_all | solution.py:87
  299.6 25.8 %all-to-all-done.1 = bf16[16,2,4096]{2,1,0:T(2,128)(2,1)S(1)} async-done(((bf16[16,2,4096]{2,1,0:T(2,128)(2,1)}), bf16[16,2,4096]{2,1,0:T(2,128)(2,1)S(1)}, u32[]{:S(2)}, u32[]{:S(2)}) %all-to-all-start.1) | async-done | bytes 262176 | tf_op jit(solution)/shard_map/all_to_all | solution.py:87
  326.4 2.9 all-gather.6.cloned.1.call-done
  332.1 2.9 collective-permute-start
  335.1 7.7 %collective-permute-start.1 = (bf16[8,8,1024]{2,1,0:T(8,128)(2,1)S(1)}, bf16[8,8,1024]{2,1,0:T(8,128)(2,1)S(1)}, u32[]{:S(2)}, u32[]{:S(2)}) collective-permute-start(bf16[8,8,1024]{2,1,0:T(8,128)(2,1)S(1)} %get-tuple-element.16), channel_id=1, source_target_pairs={{8,0},{16,8},{24,16},{32,24},{40,32},{48,40},{56,48},{64,56},{72,6... | collective-permute-start | bytes 393224 | tf_op jit(solution)/shard_map/ppermute | solution.py:24
  342.8 59.1 %all_gather.14 = bf16[64,1024]{0,1:T(8,128)(2,1)S(1)} all-gather(bf16[64,64]{0,1:T(8,128)(2,1)S(1)} %copy.105), channel_id=1, replica_groups=mesh['dp'=4,'tm'=16,'patch'=8] {'tm'}, dimensions={1}, use_global_device_ids=true | all-gather | bytes 139264 | tf_op jit(solution)/shard_map/all_gather | solution.py:100
  404.6 73.5 %all-gather.8.cloned.1.call-done = bf16[1024,2048]{1,0:T(8,128)(2,1)} async-done(((bf16[1024,128]{1,0:T(8,128)(2,1)}), bf16[1024,2048]{1,0:T(8,128)(2,1)}) %all-gather.8.cloned.1.call-update) | async-done | bytes 4194320 | tf_op jit(solution)/shard_map/all_gather | solution.py:108
  478.2 3.7 convolution_convert_fusion.1
  485.1 4.7 constant_dynamic-slice_fusion.3
  491.4 23.8 %pmax.7 = f32[2,16,64]{2,1,0:T(8,128)S(1)} all-reduce(f32[2,16,64]{2,1,0:T(8,128)S(1)} %pad_maximum_fusion), channel_id=1, replica_groups=mesh['dp'=4,'tm'=16,'patch'=8] {'patch'}, use_global_device_ids=true, to_apply=%region_10.11 | all-reduce | flops 2048 | bytes 16384 | tf_op jit(solution)/shard_map/pmax | solution.py:149
  521.4 2.2 convolution_bitcast_fusion.3
  527.1 23.6 %psum.15 = f32[2,16,64]{2,1,0:T(8,128)S(1)} all-reduce(f32[2,16,64]{2,1,0:T(8,128)S(1)} %get-tuple-element.4), channel_id=1, replica_groups=mesh['dp'=4,'tm'=16,'patch'=8] {'patch'}, use_global_device_ids=true, to_apply=%region_15.16 | all-reduce | flops 2048 | bytes 16384 | tf_op jit(solution)/shard_map/psum | solution.py:151
  550.7 45.7 %all-reduce.2.cloned.1.call-done = f32[2,16,64,64]{3,2,1,0:T(8,128)} async-done(((f32[2,16,64,64]{3,2,1,0:T(8,128)}), f32[2,16,64,64]{3,2,1,0:T(8,128)}) %all-reduce.2.cloned.1.call-update) | async-done | bytes 524304 | tf_op jit(solution)/shard_map/psum | solution.py:151
  (105 shorter events, 33.3 us)
Async XLA Ops:
  7.2 291.5 %copy-start = (bf16[1024,64]{0,1:T(8,128)(2,1)S(1)}, bf16[1024,64]{0,1:T(8,128)(2,1)}, u32[]{:S(2)}) copy-start(bf16[1024,64]{0,1:T(8,128)(2,1)} %param.18) | copy-start | bytes 393220
  7.2 197.7 %all-gather.4.cloned.1.call-start = ((), (), s32[]{:S(2)}) async-start(), calls=%async_computation.2 | async-start | bytes 6684672 | tf_op jit(solution)/shard_map/all_gather | solution.py:60
  7.9 321.4 %all-gather.6.cloned.1.call-start = ((), (), s32[]{:S(2)}) async-start(), calls=%async_computation.3 | async-start | bytes 2228224 | tf_op jit(solution)/shard_map/all_gather | solution.py:91
  8.7 469.5 %all-gather.8.cloned.1.call-start = ((), (), s32[]{:S(2)}) async-start(), calls=%async_computation.4 | async-start | bytes 4456448 | tf_op jit(solution)/shard_map/all_gather | solution.py:108
  215.6 20.5 %copy-start.5 = (bf16[64,1024]{1,0:T(8,128)(2,1)S(1)}, bf16[64,1024]{1,0:T(8,128)(2,1)}, u32[]{:S(2)}) copy-start(bf16[64,1024]{1,0:T(8,128)(2,1)} %param.17) | copy-start | bytes 393220
  225.2 37.2 %all-to-all-start = ((bf16[16,2,12288]{2,1,0:T(2,128)(2,1)}), bf16[16,2,12288]{2,1,0:T(2,128)(2,1)S(1)}, u32[]{:S(2)}, u32[]{:S(2)}) async-start(bf16[16,2,12288]{2,1,0:T(2,128)(2,1)} %reshape.171), calls=%async_computation | async-start | bytes 1572864 | tf_op jit(solution)/shard_map/all_to_all | solution.py:64
  286.3 12.3 %copy-start.17 = (f32[1024]{0:T(1024)S(1)}, f32[1024]{0:T(1024)}, u32[]{:S(2)}) copy-start(f32[1024]{0:T(1024)} %param.16) | copy-start | bytes 12292
  286.3 12.7 %copy-start.19 = (s32[2]{0:T(128)S(1)}, s32[2]{0:T(128)}, u32[]{:S(2)}) copy-start(s32[2]{0:T(128)} %param.20) | copy-start | bytes 28
  288.0 41.3 %copy-start.1 = (bf16[16,8,1024]{2,1,0:T(8,128)(2,1)S(1)}, bf16[16,8,1024]{2,1,0:T(8,128)(2,1)}, u32[]{:S(2)}) copy-start(bf16[16,8,1024]{2,1,0:T(8,128)(2,1)} %param.11) | copy-start | bytes 786436
  288.0 37.4 %all-to-all-start.1 = ((bf16[16,2,4096]{2,1,0:T(2,128)(2,1)}), bf16[16,2,4096]{2,1,0:T(2,128)(2,1)S(1)}, u32[]{:S(2)}, u32[]{:S(2)}) async-start(bf16[16,2,4096]{2,1,0:T(2,128)(2,1)} %reshape.173), calls=%async_computation.1 | async-start | bytes 524288 | tf_op jit(solution)/shard_map/all_to_all | solution.py:87
  298.1 298.2 %all-reduce.2.cloned.1.call-start = ((), (), s32[]{:S(2)}) async-start(), calls=%async_computation.5 | async-start | bytes 2097152 | tf_op jit(solution)/shard_map/psum | solution.py:151
  326.1 5.8 copy-start.18
  331.4 146.7 %copy-start.2 = (bf16[128,1024]{1,0:T(8,128)(2,1)}, bf16[128,1024]{1,0:T(8,128)(2,1)S(1)}, u32[]{:S(2)}) copy-start(bf16[128,1024]{1,0:T(8,128)(2,1)S(1)} %get-tuple-element.23) | copy-start | bytes 786436
  332.1 72.4 %collective-permute-start = (bf16[8,8,1024]{2,1,0:T(8,128)(2,1)S(1)}, bf16[8,8,1024]{2,1,0:T(8,128)(2,1)S(1)}, u32[]{:S(2)}, u32[]{:S(2)}) collective-permute-start(bf16[8,8,1024]{2,1,0:T(8,128)(2,1)S(1)} %get-tuple-element.15), channel_id=1, source_target_pairs={{0,8},{8,16},{16,24},{24,32},{32,40},{40,48},{48,56},{56,64},{64,7... | collective-permute-start | bytes 393224 | tf_op jit(solution)/shard_map/ppermute | solution.py:21
  335.1 69.5 %collective-permute-start.1 = (bf16[8,8,1024]{2,1,0:T(8,128)(2,1)S(1)}, bf16[8,8,1024]{2,1,0:T(8,128)(2,1)S(1)}, u32[]{:S(2)}, u32[]{:S(2)}) collective-permute-start(bf16[8,8,1024]{2,1,0:T(8,128)(2,1)S(1)} %get-tuple-element.16), channel_id=1, source_target_pairs={{8,0},{16,8},{24,16},{32,24},{40,32},{48,40},{56,48},{64,56},{72,6... | collective-permute-start | bytes 393224 | tf_op jit(solution)/shard_map/ppermute | solution.py:24
  404.5 85.3 %copy-start.16 = (pred[16]{0:T(512)(128)(4,1)}, pred[16]{0:T(512)(128)(4,1)S(1)}, u32[]{:S(2)}) copy-start(pred[16]{0:T(512)(128)(4,1)S(1)} %get-tuple-element.31) | copy-start | bytes 52
  404.5 86.1 %copy-start.14 = (pred[16]{0:T(512)(128)(4,1)}, pred[16]{0:T(512)(128)(4,1)S(1)}, u32[]{:S(2)}) copy-start(pred[16]{0:T(512)(128)(4,1)S(1)} %get-tuple-element.30) | copy-start | bytes 52
  490.6 28.1 %copy-start.7 = (f32[16,64]{1,0:T(8,128)}, f32[16,64]{1,0:T(8,128)S(1)}, u32[]{:S(2)}) copy-start(f32[16,64]{1,0:T(8,128)S(1)} %get-tuple-element.26) | copy-start | bytes 12292
  490.6 27.6 %slice-start = ((bf16[320,2048]{1,0:T(8,128)(2,1)}), bf16[64,2048]{1,0:T(8,128)(2,1)S(1)}, s32[]{:S(2)}) async-start(bf16[320,2048]{1,0:T(8,128)(2,1)} %copy-done.4), calls=%async_computation.6 | async-start | bytes 524288 | tf_op jit(solution)/shard_map/slice | solution.py:112
  491.4 28.9 %copy-start.9 = (f32[16,64]{1,0:T(8,128)}, f32[16,64]{1,0:T(8,128)S(1)}, u32[]{:S(2)}) copy-start(f32[16,64]{1,0:T(8,128)S(1)} %get-tuple-element.24) | copy-start | bytes 12292
  521.3 3.1 copy-start.8
  521.4 3.1 copy-start.11
  521.4 3.1 copy-start.12
  521.4 3.1 copy-start.13
  (5 other events, 10.4 us)
Sparse Core Ops, SparseCore 0:
  11.1 193.7 all-gather.3
  207.8 121.4 all-gather.5
  332.3 145.8 all-gather.7
  526.1 70.2 all-reduce.1
where the time goes:
time: 607 us; the launch traced here: 606 us
  waiting for transfers between devices  369 us (61%)
  blocking collectives  106 us (17%)
  local copies, waits for them, and re-layouts  53.4 us (9%)
  starting transfers between devices  31.3 us (5%)
  matrix products  19.4 us (3%)
  between operations  16.3 us (3%)
  other arithmetic  10.3 us (2%)
    all_gather x1, waiting for transfers between devices, on_device(): lax.all_gather(qkv_weight, 'tm', axis=1, tiled=True)  193 us
    all_gather x1, waiting for transfers between devices, on_device(): lax.all_gather(kv_weight, 'tm', axis=1, tiled=True)  73.5 us
    all_gather x1, blocking collectives, on_device(): lax.all_gather(query_shard, 'tm', axis=1, tiled=True)  59.1 us
    psum x1, waiting for transfers between devices, on_device(): lax.psum((totals * factor, mixes * factor[..., None]), 'patch')  45.7 us
    all_to_all x1, waiting for transfers between devices, on_device(): lax.all_to_all(projected, 'tm', split_axis=2, concat_axis=0, tiled=True)  26.1 us
    all_to_all x1, waiting for transfers between devices, on_device(): lax.all_to_all(attended, 'tm', split_axis=0, concat_axis=2, tiled=True)  25.8 us
    pmax x1, blocking collectives, on_device(): highest = lax.pmax(maxima, 'patch')  23.8 us
    unnamed x48, local copies, waits for them, and re-layouts  23.6 us
  transfers between devices with their start and end apart: 8, of which 6 were waited for; matrix products, arithmetic and copies ran while one was open for 9% of the time, Pallas kernels for 0%

commit v1 on v0

v1 whole, which is shorter than its diff:
```python
import jax
import jax.numpy as jnp
from jax import lax
from jax.experimental import pallas as pl
from jax.experimental.pallas import tpu as pltpu
from jax.sharding import PartitionSpec as P

MESH = pl.DeviceIdType.MESH
F32 = jnp.float32
BF16 = jnp.bfloat16
D = 1024
HEAD = 64
CLIP = 16
EPS = 1e-05
NEG = -1e30
SCALE = HEAD ** (-0.5)
SLOTS = 160
NEAR_FIRST = (1, 3, 2)


def layer_norm(value, gain):
    center = value - jnp.mean(value, axis=-1, keepdims=True)
    spread = jnp.mean(center * center, axis=-1, keepdims=True)
    return center * lax.rsqrt(spread + EPS) * gain


def dot(a, b):
    return jnp.dot(a, b, preferred_element_type=F32)


def dot_nt(a, b):
    return lax.dot_general(a, b, (((1,), (1,)), ((), ())), preferred_element_type=F32)


class Copies:
    def __init__(self, send_sem, recv_sem):
        self.send_sem = send_sem
        self.recv_sem = recv_sem
        self.slots = {}
        self.started = []

    def slot(self, name):
        return self.slots.setdefault(name, len(self.slots))

    def make(self, name, src, dst, device):
        slot = self.slot(name)
        return pltpu.make_async_remote_copy(
            src_ref=src,
            dst_ref=dst,
            send_sem=self.send_sem.at[slot],
            recv_sem=self.recv_sem.at[slot],
            device_id=device,
            device_id_type=MESH,
        )

    def send(self, name, src, dst, device):
        copy = self.make(name, src, dst, device)
        copy.start()
        self.started.append(copy)

    def wait(self, name, dst, device):
        self.make(name, dst, dst, device).wait_recv()

    def drain(self):
        for copy in self.started:
            copy.wait_send()


def kernel(
    starts_ref,
    valid_ref,
    tokens_ref,
    frame_gain_ref,
    qkv_ref,
    out_w_ref,
    pool_gain_ref,
    latent_gain_ref,
    latents_ref,
    query_w_ref,
    kv_w_ref,
    temporal_ref,
    pooled_ref,
    own_rows,
    rows,
    normed,
    wqkv,
    wout,
    wkv,
    att_out,
    att_in,
    summed,
    back,
    latn,
    held_queries,
    start_out,
    start_in,
    part_out,
    part_in,
    stat_out,
    stat_in,
    near_out,
    near_in,
    nstat_out,
    nstat_in,
    piece_out,
    piece_in,
    send_sem,
    recv_sem,
):
    t = lax.axis_index("tm")
    q = lax.axis_index("patch")
    y, g = t // 4, t % 4
    x, c = q // 2, q % 2
    copies = Copies(send_sem, recv_sem)

    def at_z(d):
        return (g + d) % 4

    def at_y(d):
        return (y + d) % 4

    def at_x(d):
        return ((x + d) % 4) * 2 + c

    def to_z(d):
        return {"tm": y * 4 + at_z(d)}

    def to_y(d):
        return {"tm": at_y(d) * 4 + g}

    def to_x(d):
        return {"patch": at_x(d)}

    def to_patch(d):
        return {"patch": (q + d) % 8}

    sibling = {"patch": x * 2 + 1 - c}
    after = {"tm": (t + 1) % 16}
    before = {"tm": (t + 15) % 16}

    barrier = pltpu.get_barrier_semaphore()
    partners = (
        [to_z(d) for d in (1, 2, 3)]
        + [to_y(d) for d in (1, 2, 3)]
        + [to_patch(d) for d in range(1, 8)]
        + [after, before]
    )
    for partner in partners:
        pl.semaphore_signal(barrier, inc=1, device_id=partner, device_id_type=MESH)

    to_row = lax.broadcasted_iota(jnp.int32, (128, 128), 0)
    from_row = lax.broadcasted_iota(jnp.int32, (128, 128), 1)
    by_position = jnp.where(from_row == (to_row & 15) * 8 + (to_row >> 4), 1.0, 0.0).astype(BF16)
    by_frame = jnp.where(from_row == (to_row & 7) * 16 + (to_row >> 3), 1.0, 0.0).astype(BF16)
    for half in range(2):
        cols = slice(half * 512, half * 512 + 512)
        own_rows[:, :, cols] = dot(by_position, tokens_ref[:, cols]).astype(BF16).reshape(4, 32, 512)

    value_cols = jnp.concatenate(
        [qkv_ref[0:512, 128:192].astype(F32), qkv_ref[512:1024, 128:192].astype(F32)], axis=1
    ).astype(BF16)
    wqkv[:, g] = jnp.concatenate([qkv_ref[:, 0:128], value_cols], axis=0).reshape(8, 192, 128)

    pl.semaphore_wait(barrier, len(partners))

    for d in (1, 3, 2):
        copies.send(f"rows{d}", own_rows.at[at_z(d)], rows.at[g], to_z(d))
    for d in NEAR_FIRST:
        copies.send(f"wqkv_z{d}", wqkv.at[q, g], wqkv.at[q, g], to_z(d))

    eighth = pl.ds(pl.multiple_of(q * 128, 128), 128)
    wout[q, t] = out_w_ref[:, eighth]
    for d in NEAR_FIRST:
        copies.send(f"wout_z{d}", wout.at[q, t], wout.at[q, t], to_z(d))

    latn[...] = layer_norm(latents_ref[...].astype(F32), latent_gain_ref[...]).astype(BF16)
    queries = dot(latn[...], query_w_ref[...])
    held_queries[...] = jnp.concatenate([queries, queries], axis=1).astype(BF16).reshape(4, 16, 128)
    wkv[q, t, 0:128, :] = kv_w_ref[eighth, :]
    wkv[q, t, 128:144, :] = held_queries[q // 2]
    for d in NEAR_FIRST:
        copies.send(f"wkv_z{d}", wkv.at[q, t], wkv.at[q, t], to_z(d))

    lane = lax.broadcasted_iota(jnp.int32, (8, 128), 1)
    start_out[...] = jnp.where(lane < 64, starts_ref[0], starts_ref[1])
    copies.send("start_after", start_out, start_in.at[0], after)
    copies.send("start_before", start_out, start_in.at[1], before)

    frame_gain = frame_gain_ref[...]

    def spread_rows(source):
        shard = y * 4 + source
        normed[shard] = layer_norm(rows[source].astype(F32), frame_gain).astype(BF16)
        for d in NEAR_FIRST:
            copies.send(("normed", d, spread_rows.count), normed.at[shard], normed.at[shard], to_y(d))
        spread_rows.count += 1

    spread_rows.count = 0
    rows[g] = own_rows[g]
    spread_rows(g)
    for d in NEAR_FIRST:
        copies.wait(f"rows{d}", rows.at[at_z(-d)], to_z(d))
        spread_rows(at_z(-d))

    def unit_start(name, buf, part):
        copies.send((name, "right"), part(buf, q), part(buf, q), to_x(1))
        copies.send((name, "left"), part(buf, q), part(buf, q), to_x(-1))
        copies.send((name, "core", 0), part(buf, q), part(buf, q), sibling)

    def unit_relay(name, buf, part, low, high):
        copies.wait((name, "right"), part(buf, at_x(-1)), to_x(1))
        copies.send((name, "relay_right"), low(buf, at_x(-1)), low(buf, at_x(-1)), to_x(1))
        copies.send((name, "core", 1), part(buf, at_x(-1)), part(buf, at_x(-1)), sibling)
        copies.wait((name, "left"), part(buf, at_x(1)), to_x(-1))
        copies.send((name, "relay_left"), high(buf, at_x(1)), high(buf, at_x(1)), to_x(-1))
        copies.send((name, "core", 2), part(buf, at_x(1)), part(buf, at_x(1)), sibling)

    def unit_far(name, buf, part, low, high):
        copies.wait((name, "relay_right"), low(buf, at_x(2)), to_x(1))
        copies.wait((name, "relay_left"), high(buf, at_x(2)), to_x(-1))
        copies.send((name, "core", 3), part(buf, at_x(2)), part(buf, at_x(2)), sibling)

    def unit_end(name, buf, part):
        for number, d in enumerate((0, -1, 1, 2)):
            other = ((x + d) % 4) * 2 + 1 - c
            copies.wait((name, "core", number), part(buf, other), sibling)

    def qkv_unit(d):
        shard = at_z(-d)
        return (
            ("wqkv", d),
            wqkv,
            lambda buf, at: buf.at[at, shard],
            lambda buf, at: buf.at[at, shard, pl.ds(0, 96)],
            lambda buf, at: buf.at[at, shard, pl.ds(96, 96)],
        )

    def y_unit(name, buf, d):
        first = at_y(-d) * 4
        return (
            (name, d),
            buf,
            lambda buf, at: buf.at[at, pl.ds(first, 4)],
            lambda buf, at: buf.at[at, pl.ds(first, 2)],
            lambda buf, at: buf.at[at, pl.ds(first + 2, 2)],
        )

    out_units = [y_unit("wout", wout, d) for d in (0, 1, 3, 2)]
    kv_units = [y_unit("wkv", wkv, d) for d in (0, 1, 3, 2)]
    qkv_units = [qkv_unit(d) for d in NEAR_FIRST]

    def over_y(name, buf):
        for d in NEAR_FIRST:
            copies.wait(f"{name}_z{d}", buf.at[q, y * 4 + at_z(-d)], to_z(d))
        part = buf.at[q, pl.ds(y * 4, 4)]
        for d in NEAR_FIRST:
            copies.send((name, "y", d), part, part, to_y(d))

    def from_y(name, buf, units):
        for d, unit in zip(NEAR_FIRST, units[1:]):
            copies.wait((name, "y", d), buf.at[q, pl.ds(at_y(-d) * 4, 4)], to_y(d))
            unit_start(*unit[:3])

    for d, unit in zip(NEAR_FIRST, qkv_units):
        copies.wait(f"wqkv_z{d}", wqkv.at[q, at_z(-d)], to_z(d))
        unit_start(*unit[:3])
    over_y("wout", wout)
    unit_start(*out_units[0][:3])
    for unit in qkv_units:
        unit_relay(*unit)
    over_y("wkv", wkv)
    unit_start(*kv_units[0][:3])
    for unit in qkv_units:
        unit_far(*unit)
    from_y("wout", wout, out_units)

    for number in range(4):
        source = (0, 1, 3, 2)[number]
        for d in NEAR_FIRST:
            shard = at_y(-d) * 4 + at_z(-source)
            copies.wait(("normed", d, number), normed.at[shard], to_y(d))
    for unit in qkv_units:
        unit_end(*unit[:3])

    valid = valid_ref[0]
    key_live = lax.broadcasted_iota(jnp.int32, (256, 256), 1) < valid

    def attend(position):
        here = normed[:, position * 16 : position * 16 + 16, :].reshape(256, D)
        for pair in range(2):
            first = wqkv[:, 2 * pair].reshape(1536, 128)
            second = wqkv[:, 2 * pair + 1].reshape(1536, 128)
            both = jnp.concatenate([first, second], axis=1)
            query_key = dot(here, both[0:1024])
            value_low = dot(here[:, 0:512], both[1024:1536])
            value_high = dot(here[:, 512:1024], both[1024:1536])
            mixed = []
            for head in range(2):
                lo = slice(head * 128, head * 128 + 64)
                hi = slice(head * 128 + 64, head * 128 + 128)
                query = query_key[:, lo].astype(BF16)
                key = query_key[:, hi].astype(BF16)
                value = (value_low[:, lo] + value_high[:, hi]).astype(BF16)
                scores = jnp.where(key_live, dot_nt(query, key) * SCALE, -jnp.inf)
                weights = jnp.exp(scores - jnp.max(scores, axis=-1, keepdims=True))
                total = jnp.sum(weights, axis=-1, keepdims=True)
                mixed.append(dot(weights.astype(BF16), value) / total)
            result = jnp.concatenate(mixed, axis=1).astype(BF16).reshape(4, 4, 16, 128)
            for source in range(4):
                at = source * 32 + position * 16
                att_out[:, at : at + 16, pair * 128 : pair * 128 + 128] = result[:, source]

    attend(0)
    for unit in out_units:
        unit_relay(*unit)
    attend(1)
    for d in NEAR_FIRST:
        copies.send(f"att{d}", att_out.at[at_y(d)], att_in.at[y], to_y(d))
    att_in[y] = att_out[y]
    for unit in out_units:
        unit_far(*unit)
    from_y("wkv", wkv, kv_units)
    for unit in out_units:
        unit_end(*unit[:3])
    for d in NEAR_FIRST:
        copies.wait(f"att{d}", att_in.at[at_y(-d)], to_y(d))

    attended = jnp.concatenate([att_in[source] for source in range(4)], axis=1)
    for block in range(4):
        weight = jnp.concatenate(
            [wout[2 * block].reshape(D, 128), wout[2 * block + 1].reshape(D, 128)], axis=1
        )
        cols = slice(block * 256, block * 256 + 256)
        total = rows[:, :, cols].astype(F32).reshape(128, 256) + dot(attended, weight)
        summed[:, :, cols] = total.astype(BF16).reshape(4, 32, 256)
    for d in NEAR_FIRST:
        copies.send(f"back{d}", summed.at[at_z(d)], back.at[g], to_z(d))
    back[g] = summed[g]

    for unit in kv_units:
        unit_relay(*unit)
    for unit in kv_units:
        unit_far(*unit)

    copies.wait("start_after", start_in.at[0], after)
    copies.wait("start_before", start_in.at[1], before)
    starts_far = jnp.where(lane < 64, start_in[1], start_in[0])[0:1]
    starts_own = start_out[0:1, :]
    row = lax.broadcasted_iota(jnp.int32, (128, 128), 0)
    frame = t * 16 + (row & 15)
    live = [
        (frame >= starts) & (frame < starts + CLIP) & (frame < valid)
        for starts in (starts_own, starts_far)
    ]

    for d in NEAR_FIRST:
        copies.wait(f"back{d}", back.at[at_z(-d)], to_z(d))
    held = back[...].reshape(128, D)
    pooled = layer_norm(held.astype(F32), pool_gain_ref[...]).astype(BF16)
    for half in range(2):
        cols = slice(half * 512, half * 512 + 512)
        temporal_ref[:, cols] = dot(by_frame, held[:, cols]).astype(BF16)
    for unit in kv_units:
        unit_end(*unit[:3])

    def head_queries(head):
        own = [wkv[2 * block, head, 128:144, :] for block in range(4)]
        return jnp.concatenate(own + own, axis=0)[:, 0:64]

    def pool_pair(pair, part_ref, stat_ref):
        weight = jnp.concatenate(
            [
                wkv[:, 2 * pair, 0:128, :].reshape(D, 128),
                wkv[:, 2 * pair + 1, 0:128, :].reshape(D, 128),
            ],
            axis=1,
        )
        pair_kv = dot(pooled, weight)
        for head in range(2):
            own_kv = pair_kv[:, head * 128 : head * 128 + 128]
            key = own_kv[:, 0:64].astype(BF16)
            value_t = jnp.transpose(own_kv)[64:128, :].astype(BF16)
            scores = dot_nt(key, head_queries(2 * pair + head)) * SCALE
            for side in range(2):
                cols = slice(side * 128, side * 128 + 128)
                top = jnp.max(jnp.where(live[side], scores, NEG), axis=0, keepdims=True)
                weights = jnp.where(live[side], jnp.exp(scores - top), 0.0)
                stat_ref[head : head + 1, cols] = top
                stat_ref[head + 2 : head + 3, cols] = jnp.sum(weights, axis=0, keepdims=True)
                part_ref[head * 64 : head * 64 + 64, cols] = dot(
                    value_t, weights.astype(BF16)
                ).astype(BF16)

    stat_out[...] = jnp.zeros_like(stat_out)
    stat_in[q] = jnp.zeros((8, 256), F32)
    for d in range(1, 8):
        to = (q + d) % 8
        pool_pair(to, part_out.at[to], stat_out.at[to])
        copies.send(("part", d), part_out.at[to], part_in.at[q], to_patch(d))
        copies.send(("stat", d), stat_out.at[to], stat_in.at[q], to_patch(d))
    pool_pair(q, part_in.at[q], stat_in.at[q])

    self_scores, self_values = [], []
    for head in range(2):
        weight = wkv[:, 2 * q + head, 0:128, :].reshape(D, 128)
        own_kv = dot(latn[...], weight)
        key = own_kv[:, 0:64].astype(BF16)
        self_values.append(own_kv[:, 64:128].astype(BF16))
        self_scores.append(dot_nt(key, head_queries(2 * q + head)) * SCALE)

    for d in range(1, 8):
        source = (q + 8 - d) % 8
        copies.wait(("part", d), part_in.at[source], to_patch(d))
        copies.wait(("stat", d), stat_in.at[source], to_patch(d))
    tops = [stat_in[source] for source in range(8)]
    highest = tops[0]
    for top in tops[1:]:
        highest = jnp.maximum(highest, top)
    mixes = []
    nstat_out[...] = jnp.zeros_like(nstat_out)
    own_tops, own_totals = [], []
    for head in range(2):
        top = highest[head : head + 1]
        total = jnp.zeros((1, 256), F32)
        mix = jnp.zeros((64, 256), F32)
        for source in range(8):
            factor = jnp.exp(tops[source][head : head + 1] - top)
            total += tops[source][head + 2 : head + 3] * factor
            mix += part_in[source, head * 64 : head * 64 + 64, :].astype(F32) * factor
        own_tops.append(top[:, 0:128])
        own_totals.append(total[:, 0:128])
        mixes.append(mix[:, 0:128])
        near_out[head * 64 : head * 64 + 64, :] = mix[:, 128:256].astype(BF16)
        nstat_out[head : head + 1, :] = top[:, 128:256]
        nstat_out[head + 2 : head + 3, :] = total[:, 128:256]
    copies.send("near_after", near_out, near_in.at[0], after)
    copies.send("nstat_after", nstat_out, nstat_in.at[0], after)
    copies.send("near_before", near_out, near_in.at[1], before)
    copies.send("nstat_before", nstat_out, nstat_in.at[1], before)
    copies.wait("near_after", near_in.at[0], after)
    copies.wait("nstat_after", nstat_in.at[0], after)
    copies.wait("near_before", near_in.at[1], before)
    copies.wait("nstat_before", nstat_in.at[1], before)

    near_stat = jnp.where(lane < 64, nstat_in[0], nstat_in[1])
    wide_lane = lax.broadcasted_iota(jnp.int32, (64, 128), 1)
    results = []
    for head in range(2):
        span = slice(head * 64, head * 64 + 64)
        near_mix = jnp.where(wide_lane < 64, near_in[0, span].astype(F32), near_in[1, span].astype(F32))
        near_top = near_stat[head : head + 1]
        near_total = near_stat[head + 2 : head + 3]
        scores = self_scores[head]
        top = jnp.maximum(
            jnp.maximum(own_tops[head], near_top), jnp.max(scores, axis=0, keepdims=True)
        )
        own_factor = jnp.exp(own_tops[head] - top)
        near_factor = jnp.exp(near_top - top)
        weights = jnp.exp(scores - top)
        total = (
            own_totals[head] * own_factor
            + near_total * near_factor
            + jnp.sum(weights, axis=0, keepdims=True)
        )
        self_mix = lax.dot_general(
            self_values[head],
            weights.astype(BF16),
            (((0,), (0,)), ((), ())),
            preferred_element_type=F32,
        )
        results.append((mixes[head] * own_factor + near_mix * near_factor + self_mix) / total)
    piece = jnp.transpose(jnp.concatenate(results, axis=0)).astype(BF16)
    piece_out[...] = piece
    for d in range(1, 8):
        copies.send(("piece", d), piece_out, piece_in.at[q], to_patch(d))
    piece_in[q] = piece
    for d in range(1, 8):
        copies.wait(("piece", d), piece_in.at[(q + 8 - d) % 8], to_patch(d))
    for block in range(8):
        pooled_ref[:, block * 128 : block * 128 + 128] = piece_in[block]
    copies.drain()
    assert len(copies.slots) <= SLOTS


def on_device(
    tokens,
    frame_gain,
    qkv_weight,
    out_weight,
    pool_gain,
    latent_gain,
    latents,
    query_weight,
    kv_weight,
    clip_starts,
    valid_frames,
):
    frames_dev, patch_dev, width = tokens.shape
    vmem = pl.BlockSpec(memory_space=pltpu.VMEM)
    smem = pl.BlockSpec(memory_space=pltpu.SMEM)
    temporal_out, pooled = pl.pallas_call(
        kernel,
        out_shape=(
            jax.ShapeDtypeStruct((128, D), BF16),
            jax.ShapeDtypeStruct((128, D), BF16),
        ),
        in_specs=[smem, smem] + [vmem] * 9,
        out_specs=(vmem, vmem),
        scratch_shapes=[
            pltpu.VMEM((4, 32, D), BF16),
            pltpu.VMEM((4, 32, D), BF16),
            pltpu.VMEM((16, 32, D), BF16),
            pltpu.VMEM((8, 4, 192, 128), BF16),
            pltpu.VMEM((8, 16, 64, 128), BF16),
            pltpu.VMEM((8, 16, 144, 128), BF16),
            pltpu.VMEM((4, 128, 256), BF16),
            pltpu.VMEM((4, 128, 256), BF16),
            pltpu.VMEM((4, 32, D), BF16),
            pltpu.VMEM((4, 32, D), BF16),
            pltpu.VMEM((64, D), BF16),
            pltpu.VMEM((4, 16, 128), BF16),
            pltpu.VMEM((8, 128), jnp.int32),
            pltpu.VMEM((2, 8, 128), jnp.int32),
            pltpu.VMEM((8, 128, 256), BF16),
            pltpu.VMEM((8, 128, 256), BF16),
            pltpu.VMEM((8, 8, 256), F32),
            pltpu.VMEM((8, 8, 256), F32),
            pltpu.VMEM((128, 128), BF16),
            pltpu.VMEM((2, 128, 128), BF16),
            pltpu.VMEM((8, 128), F32),
            pltpu.VMEM((2, 8, 128), F32),
            pltpu.VMEM((128, 128), BF16),
            pltpu.VMEM((8, 128, 128), BF16),
            pltpu.SemaphoreType.DMA((SLOTS,)),
            pltpu.SemaphoreType.DMA((SLOTS,)),
        ],
        compiler_params=pltpu.CompilerParams(
            collective_id=0, has_side_effects=True, vmem_limit_bytes=48 * 1024 * 1024
        ),
    )(
        clip_starts,
        valid_frames,
        tokens.reshape(frames_dev * patch_dev, width),
        frame_gain.reshape(1, width),
        qkv_weight,
        out_weight,
        pool_gain.reshape(1, width),
        latent_gain.reshape(1, width),
        latents,
        query_weight,
        kv_weight,
    )
    return (
        temporal_out.reshape(frames_dev, patch_dev, width),
        pooled.reshape(2, 64, width),
    )


def solution(mesh):
    in_specs = (
        P(("dp", "tm"), "patch", None),
        P(),
        P(None, "tm"),
        P("tm", None),
        P(),
        P(),
        P(),
        P(None, "tm"),
        P(None, "tm"),
        P(("dp", "tm")),
        P("dp"),
    )
    out_specs = (P(("dp", "tm"), "patch", None), P(("dp", "tm"), None, None))
    return jax.shard_map(
        on_device, mesh=mesh, in_specs=in_specs, out_specs=out_specs, check_vma=False
    )
```

time: 607 us -> 113 us (0.19)
  the two profiles are of different devices: /device:TPU:8 before, /device:TPU:33 now
where the time goes in v1:
time: 113 us
  Pallas kernels  108 us (96%)
  local copies, waits for them, and re-layouts  3.53 us (3%)
  between operations  1.43 us (1%)
    pallas_call x1, Pallas kernels, on_device(): pl.pallas_call(kernel, out_shape=(jax.ShapeDtypeStruct((128, D), BF16), j...  108 us
    unnamed x22, local copies, waits for them, and re-layouts  3.53 us

profile of v1, /device:TPU:33, one launch (start us, length us, event | category | flops | bytes accessed | tf_op | source)
XLA Modules:
  0.0 113.3 jit_solution(17412597540387848796)
XLA Ops:
  0.6 0.0 copy-start.8
  1.3 1.1 copy.14.query_w_ref
  2.4 0.0 copy-done.8
  2.4 0.0 copy-start
  2.4 0.0 copy-start.1
  2.4 0.0 copy-start.2
  2.5 0.0 copy-start.3
  2.5 0.0 copy-start.4
  2.5 0.0 copy-start.5
  2.5 0.0 copy-start.6
  2.5 0.0 copy-start.7
  2.5 0.2 copy.13.qkv_ref
  2.7 0.6 copy-done
  3.4 0.1 copy-done.1
  3.5 0.0 copy-done.2
  3.5 0.0 copy-done.3
  3.5 0.0 copy-done.4
  3.5 0.0 copy-done.5
  3.5 0.0 copy-done.6
  3.5 0.0 copy-done.7
  3.5 108.3 %shard_map.122 = (bf16[128,1024]{1,0:T(8,128)(2,1)S(1)}, bf16[128,1024]{1,0:T(8,128)(2,1)S(1)}) custom-call(s32[2]{0:T(128)S(1)} %copy-done.7, s32[1]{0:T(128)S(6)} %copy.17.valid_ref, bf16[128,1024]{1,0:T(8,128)(2,1)S(1)} %bitcast.8, f32[1,1024]{1,0:T(1,128)S(1)} %bitcast.9, bf16[1024,192]{1,0:T(8,128)(2,1)S(1)} %copy.13.qkv_ref, ...), custom_call_target="tpu_custom_call" | custom-call | tf_op jit(solution)/shard_map/pallas_call | solution.py:501
  111.9 0.7 copy.18
  112.6 0.7 copy.19
Async XLA Ops:
  0.6 1.8 %copy-start.8 = (bf16[1024,192]{0,1:T(8,128)(2,1)S(1)}, bf16[1024,192]{0,1:T(8,128)(2,1)}, u32[]{:S(2)}) copy-start(bf16[1024,192]{0,1:T(8,128)(2,1)} %param.13) | copy-start | bytes 1179652
  2.4 1.0 copy-start
  2.4 1.0 copy-start.1
  2.4 1.0 copy-start.2
  2.5 1.1 copy-start.3
  2.5 1.1 copy-start.4
  2.5 1.1 copy-start.5
  2.5 1.0 copy-start.6
  2.5 1.0 copy-start.7

commit v2 on v1

v2 whole, which is shorter than its diff:
```python
import jax
import jax.numpy as jnp
from jax import lax
from jax.experimental import pallas as pl
from jax.experimental.pallas import tpu as pltpu
from jax.sharding import PartitionSpec as P

MESH = pl.DeviceIdType.MESH
F32 = jnp.float32
BF16 = jnp.bfloat16
D = 1024
HEAD = 64
CLIP = 16
EPS = 1e-05
NEG = -1e30
SCALE = HEAD ** (-0.5)
SLOTS = 160
NEAR_FIRST = (1, 3, 2)


def layer_norm(value, gain):
    center = value - jnp.mean(value, axis=-1, keepdims=True)
    spread = jnp.mean(center * center, axis=-1, keepdims=True)
    return center * lax.rsqrt(spread + EPS) * gain


def dot(a, b):
    return jnp.dot(a, b, preferred_element_type=F32)


def dot_nt(a, b):
    return lax.dot_general(a, b, (((1,), (1,)), ((), ())), preferred_element_type=F32)


class Copies:
    def __init__(self, send_sem, recv_sem):
        self.send_sem = send_sem
        self.recv_sem = recv_sem
        self.slots = {}
        self.started = []

    def slot(self, name):
        return self.slots.setdefault(name, len(self.slots))

    def make(self, name, src, dst, device):
        slot = self.slot(name)
        return pltpu.make_async_remote_copy(
            src_ref=src,
            dst_ref=dst,
            send_sem=self.send_sem.at[slot],
            recv_sem=self.recv_sem.at[slot],
            device_id=device,
            device_id_type=MESH,
        )

    def send(self, name, src, dst, device):
        copy = self.make(name, src, dst, device)
        copy.start()
        self.started.append(copy)

    def wait(self, name, dst, device):
        self.make(name, dst, dst, device).wait_recv()

    def drain(self):
        for copy in self.started:
            copy.wait_send()


def kernel(
    starts_ref,
    valid_ref,
    tokens_ref,
    frame_gain_ref,
    qkv_ref,
    out_w_ref,
    pool_gain_ref,
    latent_gain_ref,
    latents_ref,
    query_w_ref,
    kv_w_ref,
    temporal_ref,
    pooled_ref,
    own_rows,
    rows,
    normed,
    wqkv,
    wout,
    wkv,
    att_out,
    att_in,
    summed,
    back,
    pooled,
    latn,
    held_queries,
    block_queries,
    keys,
    values,
    start_out,
    start_in,
    part_out,
    part_in,
    stat_out,
    stat_in,
    near_out,
    near_in,
    nstat_out,
    nstat_in,
    piece_out,
    piece_in,
    send_sem,
    recv_sem,
):
    t = lax.axis_index("tm")
    q = lax.axis_index("patch")
    y, g = t // 4, t % 4
    x, c = q // 2, q % 2
    copies = Copies(send_sem, recv_sem)

    def at_z(d):
        return (g + d + 4) % 4

    def at_y(d):
        return (y + d + 4) % 4

    def at_x(d):
        return ((x + d + 4) % 4) * 2 + c

    def to_z(d):
        return {"tm": y * 4 + at_z(d)}

    def to_y(d):
        return {"tm": at_y(d) * 4 + g}

    def to_x(d):
        return {"patch": at_x(d)}

    def to_patch(d):
        return {"patch": (q + d) % 8}

    sibling = {"patch": x * 2 + 1 - c}
    after = {"tm": (t + 1) % 16}
    before = {"tm": (t + 15) % 16}

    barrier = pltpu.get_barrier_semaphore()
    partners = (
        [to_z(d) for d in (1, 2, 3)]
        + [to_y(d) for d in (1, 2, 3)]
        + [to_patch(d) for d in range(1, 8)]
        + [after, before]
    )
    for partner in partners:
        pl.semaphore_signal(barrier, inc=1, device_id=partner, device_id_type=MESH)

    to_row = lax.broadcasted_iota(jnp.int32, (128, 128), 0)
    from_row = lax.broadcasted_iota(jnp.int32, (128, 128), 1)
    by_position = jnp.where(from_row == (to_row & 15) * 8 + (to_row >> 4), 1.0, 0.0).astype(BF16)
    for half in range(2):
        cols = slice(half * 512, half * 512 + 512)
        own_rows[:, :, cols] = dot(by_position, tokens_ref[:, cols]).astype(BF16).reshape(4, 32, 512)
    for block in range(8):
        wqkv[block, g] = qkv_ref[:, block * 128 : block * 128 + 128]

    pl.semaphore_wait(barrier, len(partners))

    for d in NEAR_FIRST:
        copies.send(f"wqkv_z{d}", wqkv.at[q, g], wqkv.at[q, g], to_z(d))
    for d in NEAR_FIRST:
        copies.send(f"rows{d}", own_rows.at[at_z(d)], rows.at[g], to_z(d))

    lane = lax.broadcasted_iota(jnp.int32, (8, 128), 1)
    start_out[...] = jnp.where(lane < 64, starts_ref[0], starts_ref[1])
    copies.send("start_after", start_out, start_in.at[0], after)
    copies.send("start_before", start_out, start_in.at[1], before)

    frame_gain = frame_gain_ref[...]

    def spread_rows(number, source):
        shard = y * 4 + source
        normed[shard] = layer_norm(rows[source].astype(F32), frame_gain).astype(BF16)
        for d in NEAR_FIRST:
            copies.send(("normed", d, number), normed.at[shard], normed.at[shard], to_y(d))

    rows[g] = own_rows[g]
    spread_rows(0, g)

    eighth = pl.ds(pl.multiple_of(q * 128, 128), 128)
    wout[q, t] = out_w_ref[:, eighth]

    latn[...] = layer_norm(latents_ref[...].astype(F32), latent_gain_ref[...]).astype(BF16)
    queries = dot_nt(query_w_ref[...], latn[...])
    held_queries[...] = jnp.concatenate([queries, queries], axis=1).astype(BF16).reshape(4, 16, 128)
    wkv[q, t, 0:128, :] = jnp.transpose(kv_w_ref[eighth, :].astype(F32)).astype(BF16)
    wkv[q, t, 128:144, :] = held_queries[q // 2]

    def unit_start(name, buf, part):
        copies.send((name, "right"), part(buf, q), part(buf, q), to_x(1))
        copies.send((name, "left"), part(buf, q), part(buf, q), to_x(-1))
        copies.send((name, "core", 0), part(buf, q), part(buf, q), sibling)

    def unit_relay(name, buf, part, low, high):
        copies.wait((name, "right"), part(buf, at_x(-1)), to_x(1))
        copies.send((name, "relay_right"), low(buf, at_x(-1)), low(buf, at_x(-1)), to_x(1))
        copies.send((name, "core", 1), part(buf, at_x(-1)), part(buf, at_x(-1)), sibling)
        copies.wait((name, "left"), part(buf, at_x(1)), to_x(-1))
        copies.send((name, "relay_left"), high(buf, at_x(1)), high(buf, at_x(1)), to_x(-1))
        copies.send((name, "core", 2), part(buf, at_x(1)), part(buf, at_x(1)), sibling)

    def unit_far(name, buf, part, low, high):
        copies.wait((name, "relay_right"), low(buf, at_x(2)), to_x(1))
        copies.wait((name, "relay_left"), high(buf, at_x(2)), to_x(-1))
        copies.send((name, "core", 3), part(buf, at_x(2)), part(buf, at_x(2)), sibling)

    def unit_end(name, buf, part):
        for number, d in enumerate((0, -1, 1, 2)):
            other = ((x + d + 4) % 4) * 2 + 1 - c
            copies.wait((name, "core", number), part(buf, other), sibling)

    def qkv_unit(d):
        shard = at_z(-d)
        return (
            ("wqkv", d),
            wqkv,
            lambda buf, at: buf.at[at, shard],
            lambda buf, at: buf.at[at, shard, pl.ds(0, 96)],
            lambda buf, at: buf.at[at, shard, pl.ds(96, 96)],
        )

    def y_unit(name, buf, d):
        first = at_y(-d) * 4
        return (
            (name, d),
            buf,
            lambda buf, at: buf.at[at, pl.ds(first, 4)],
            lambda buf, at: buf.at[at, pl.ds(first, 2)],
            lambda buf, at: buf.at[at, pl.ds(first + 2, 2)],
        )

    out_units = [y_unit("wout", wout, d) for d in (0, 1, 3, 2)]
    kv_units = [y_unit("wkv", wkv, d) for d in (0, 1, 3, 2)]
    qkv_units = [qkv_unit(d) for d in NEAR_FIRST]

    def over_z(name, buf):
        for d in NEAR_FIRST:
            copies.send(f"{name}_z{d}", buf.at[q, t], buf.at[q, t], to_z(d))

    def over_y(name, buf):
        for d in NEAR_FIRST:
            copies.wait(f"{name}_z{d}", buf.at[q, y * 4 + at_z(-d)], to_z(d))
        part = buf.at[q, pl.ds(y * 4, 4)]
        for d in NEAR_FIRST:
            copies.send((name, "y", d), part, part, to_y(d))

    def from_y(name, buf, units):
        for d, unit in zip(NEAR_FIRST, units[1:]):
            copies.wait((name, "y", d), buf.at[q, pl.ds(at_y(-d) * 4, 4)], to_y(d))
            unit_start(*unit[:3])

    for d, unit in zip(NEAR_FIRST, qkv_units):
        copies.wait(f"wqkv_z{d}", wqkv.at[q, at_z(-d)], to_z(d))
        unit_start(*unit[:3])
    for number, d in ((1, 1), (2, 3)):
        copies.wait(f"rows{d}", rows.at[at_z(-d)], to_z(d))
        spread_rows(number, at_z(-d))
    for unit in qkv_units:
        unit_relay(*unit)
    copies.wait("rows2", rows.at[at_z(-2)], to_z(2))
    spread_rows(3, at_z(-2))
    over_z("wout", wout)
    over_z("wkv", wkv)
    for unit in qkv_units:
        unit_far(*unit)
    for number, source in enumerate((0, 1, 3, 2)):
        for d in NEAR_FIRST:
            shard = at_y(-d) * 4 + at_z(-source)
            copies.wait(("normed", d, number), normed.at[shard], to_y(d))
    for unit in qkv_units:
        unit_end(*unit[:3])

    valid = valid_ref[0]
    key_live = lax.broadcasted_iota(jnp.int32, (256, 256), 1) < valid
    first_head = lax.broadcasted_iota(jnp.int32, (256, 128), 1) < 64

    def attend(position):
        here = normed[:, position * 16 : position * 16 + 16, :].reshape(256, D)
        for pair in range(2):
            blocks = []
            for block in range(8):
                parts = [
                    wqkv[block, 2 * pair + head, kind * 64 : kind * 64 + 64, :]
                    for kind in range(3)
                    for head in range(2)
                ]
                blocks.append(jnp.concatenate(parts, axis=0))
            weight = jnp.concatenate(blocks, axis=1)
            projected = dot_nt(here, weight).astype(BF16)
            query, key, value = (projected[:, k * 128 : k * 128 + 128] for k in range(3))
            mixed = []
            for head in range(2):
                mine = first_head if head == 0 else jnp.logical_not(first_head)
                scores = dot_nt(jnp.where(mine, query, jnp.zeros_like(query)), key) * SCALE
                scores = jnp.where(key_live, scores, -jnp.inf)
                weights = jnp.exp(scores - jnp.max(scores, axis=-1, keepdims=True))
                total = jnp.sum(weights, axis=-1, keepdims=True)
                mixed.append(dot(weights.astype(BF16), value) / total)
            result = jnp.where(first_head, mixed[0], mixed[1]).astype(BF16)
            att_out[position, :, :, pair * 128 : pair * 128 + 128] = result.reshape(4, 64, 128)
        for d in NEAR_FIRST:
            copies.send(
                ("att", d, position), att_out.at[position, at_y(d)], att_in.at[position, y], to_y(d)
            )
        att_in[position, y] = att_out[position, y]

    def project(position):
        for d in NEAR_FIRST:
            copies.wait(("att", d, position), att_in.at[position, at_y(-d)], to_y(d))
        attended = jnp.concatenate([att_in[position, source] for source in range(4)], axis=1)
        for block in range(4):
            weight = jnp.concatenate(
                [wout[2 * block].reshape(D, 128), wout[2 * block + 1].reshape(D, 128)], axis=1
            )
            cols = slice(block * 256, block * 256 + 256)
            tokens = rows[:, position * 16 : position * 16 + 16, cols]
            total = tokens.astype(F32).reshape(64, 256) + dot(attended, weight)
            summed[position, :, :, cols] = total.astype(BF16).reshape(4, 16, 256)
        for d in NEAR_FIRST:
            copies.send(
                ("back", d, position), summed.at[position, at_z(d)], back.at[position, g], to_z(d)
            )
        back[position, g] = summed[position, g]

    attend(0)
    over_y("wout", wout)
    unit_start(*out_units[0][:3])
    attend(1)
    over_y("wkv", wkv)
    unit_start(*kv_units[0][:3])
    from_y("wout", wout, out_units)
    for unit in out_units:
        unit_relay(*unit)
    from_y("wkv", wkv, kv_units)
    for unit in out_units:
        unit_far(*unit)
    for unit in out_units:
        unit_end(*unit[:3])
    project(0)
    project(1)

    for unit in kv_units:
        unit_relay(*unit)
    for unit in kv_units:
        unit_far(*unit)
    copies.wait("start_after", start_in.at[0], after)
    copies.wait("start_before", start_in.at[1], before)

    pool_gain = pool_gain_ref[...]

    def pool_norm(position, source):
        value = layer_norm(back[position, source].astype(F32), pool_gain)
        pooled[position, source] = value.astype(BF16)

    for position in range(2):
        pool_norm(position, g)
        for d in NEAR_FIRST:
            copies.wait(("back", d, position), back.at[position, at_z(-d)], to_z(d))
            pool_norm(position, at_z(-d))
    for unit in kv_units:
        unit_end(*unit[:3])

    wide_lane = lax.broadcasted_iota(jnp.int32, (64, 256), 1)
    for quad in range(4):
        for head in range(4):
            parts = [wkv[2 * block, 4 * quad + head, 128:144, :] for block in range(4)]
            query = jnp.concatenate(parts, axis=0)
            query = jnp.concatenate([query, query], axis=1)
            block_queries[quad, head * 64 : head * 64 + 64, :] = jnp.where(
                (wide_lane >> 6) == head, query, jnp.zeros_like(query)
            )

    far_starts = jnp.where(lane < 64, start_in[1], start_in[0])[0:1]
    own_starts = start_out[0:1, :]
    frame = t * 16 + (lax.broadcasted_iota(jnp.int32, (128, 128), 0) & 15)
    in_lane = lax.broadcasted_iota(jnp.int32, (1, 128), 1)

    def live_of(starts, second):
        half = jnp.where((in_lane >= 64) == second, starts, -(10**6))
        start = jnp.max(half, axis=1, keepdims=True)
        return (frame >= start) & (frame < start + CLIP) & (frame < valid)

    live = [
        live_of(own_starts, False),
        live_of(own_starts, True),
        live_of(far_starts, False),
        live_of(far_starts, True),
    ]
    live = [jnp.concatenate([mask, mask], axis=1) for mask in live]
    pair_lane = lax.broadcasted_iota(jnp.int32, (64, 128), 1)
    rows_now = pooled[...].reshape(128, D)

    def kv_project(quad):
        key_blocks, value_blocks = [], []
        for block in range(8):
            four = wkv[block, pl.ds(quad * 4, 4)]
            key_blocks.append(four[:, 0:64, :].reshape(256, 128))
            value_blocks.append(four[:, 64:128, :].reshape(256, 128))
        keys[quad] = dot_nt(rows_now, jnp.concatenate(key_blocks, axis=1)).astype(BF16)
        values[quad] = dot_nt(jnp.concatenate(value_blocks, axis=1), rows_now).astype(BF16)

    def pool_quad(quad):
        scores = dot(keys[quad], block_queries[quad]) * SCALE
        value = values[quad]
        for clip in range(4):
            top = jnp.max(jnp.where(live[clip], scores, NEG), axis=0, keepdims=True)
            weights = jnp.where(live[clip], jnp.exp(scores - top), 0.0)
            total = jnp.sum(weights, axis=0, keepdims=True)
            mix = dot(value, weights.astype(BF16))
            for pair in range(2):
                cols = slice(pair * 128, pair * 128 + 128)
                even = mix[pair * 128 : pair * 128 + 64, cols]
                odd = mix[pair * 128 + 64 : pair * 128 + 128, cols]
                part_out[quad, pair, clip * 64 : clip * 64 + 64, :] = jnp.where(
                    pair_lane < 64, even, odd
                ).astype(BF16)
                stat_out[quad, pair, clip : clip + 1, :] = top[:, cols]
                stat_out[quad, pair, 4 + clip : 5 + clip, :] = total[:, cols]

    def send_part(name, quad, core):
        device = {"patch": quad * 2 + core}
        copies.send(("part", name), part_out.at[quad, core], part_in.at[q], device)
        copies.send(("stat", name), stat_out.at[quad, core], stat_in.at[q], device)

    order = [(x + k) % 4 for k in (2, 1, 3, 0)]
    kv_project(order[0])
    for number, quad in enumerate(order):
        if number < 3:
            kv_project(order[number + 1])
        pool_quad(quad)
        if number < 3:
            send_part(("same", number), quad, c)
        send_part(("cross", number), quad, 1 - c)
    part_in[q] = part_out[x, c]
    stat_in[q] = stat_out[x, c]

    key_blocks, value_blocks = [], []
    for block in range(8):
        two = wkv[block, pl.ds(q * 2, 2)]
        key_blocks.append(two[:, 0:64, :].reshape(128, 128))
        value_blocks.append(two[:, 64:128, :].reshape(128, 128))
    self_key = dot_nt(latn[...], jnp.concatenate(key_blocks, axis=1)).astype(BF16)
    self_value = dot_nt(jnp.concatenate(value_blocks, axis=1), latn[...]).astype(BF16)
    pair_queries = jnp.where(
        c == 0, block_queries[x, 0:128, 0:128], block_queries[x, 128:256, 128:256]
    )
    self_scores = dot(self_key, pair_queries) * SCALE
    self_top = jnp.max(self_scores, axis=0, keepdims=True)

    by_frame = jnp.where(
        from_row == (to_row & 1) * 64 + ((to_row & 7) >> 1) * 16 + (to_row >> 3), 1.0, 0.0
    ).astype(BF16)
    held = back[...].reshape(128, D)
    for half in range(2):
        cols = slice(half * 512, half * 512 + 512)
        temporal_ref[:, cols] = dot(by_frame, held[:, cols]).astype(BF16)

    for number, k in enumerate((2, 1, 3, 0)):
        source = ((x + 4 - k) % 4) * 2
        if number < 3:
            copies.wait(("part", ("same", number)), part_in.at[source + c], to_x(k))
            copies.wait(("stat", ("same", number)), stat_in.at[source + c], to_x(k))
        copies.wait(("part", ("cross", number)), part_in.at[source + 1 - c], sibling)
        copies.wait(("stat", ("cross", number)), stat_in.at[source + 1 - c], sibling)
    stats = [stat_in[source] for source in range(8)]
    highest = stats[0][0:4]
    for stat in stats[1:]:
        highest = jnp.maximum(highest, stat[0:4])
    factors = [jnp.exp(stat[0:4] - highest) for stat in stats]
    totals = jnp.zeros((4, 128), F32)
    for stat, factor in zip(stats, factors):
        totals += stat[4:8] * factor
    nstat_out[0:4, :] = highest
    nstat_out[4:8, :] = totals

    def gathered(clip):
        mix = jnp.zeros((64, 128), F32)
        for source in range(8):
            part = part_in[source, clip * 64 : clip * 64 + 64, :].astype(F32)
            mix += part * factors[source][clip : clip + 1]
        return mix

    near_out[0] = gathered(2).astype(BF16)
    copies.send("near_after", near_out.at[0], near_in.at[0], after)
    copies.send("nstat_after", nstat_out, nstat_in.at[0], after)
    near_out[1] = gathered(3).astype(BF16)
    copies.send("near_before", near_out.at[1], near_in.at[1], before)
    copies.send("nstat_before", nstat_out, nstat_in.at[1], before)
    own_mixes = [gathered(0), gathered(1)]

    finished = []
    for clip, name, device in ((0, "after", after), (1, "before", before)):
        copies.wait(f"near_{name}", near_in.at[clip], device)
        copies.wait(f"nstat_{name}", nstat_in.at[clip], device)
        near_top = nstat_in[clip, 2 + clip : 3 + clip, :]
        near_total = nstat_in[clip, 6 + clip : 7 + clip, :]
        own_top = highest[clip : clip + 1]
        top = jnp.maximum(jnp.maximum(own_top, near_top), self_top)
        own_factor = jnp.exp(own_top - top)
        near_factor = jnp.exp(near_top - top)
        weights = jnp.exp(self_scores - top)
        total = (
            totals[clip : clip + 1] * own_factor
            + near_total * near_factor
            + jnp.sum(weights, axis=0, keepdims=True)
        )
        self_mix = dot(self_value, weights.astype(BF16))
        self_mix = jnp.where(pair_lane < 64, self_mix[0:64], self_mix[64:128])
        mix = own_mixes[clip] * own_factor + near_in[clip].astype(F32) * near_factor + self_mix
        finished.append(mix / total)

    turned = jnp.transpose(jnp.concatenate(finished, axis=0))
    even, odd = turned[0:64], turned[64:128]
    piece_out[0:64, :] = jnp.where(pair_lane < 64, even, pltpu.roll(odd, 64, 1)).astype(BF16)
    piece_out[64:128, :] = jnp.where(pair_lane < 64, pltpu.roll(even, 64, 1), odd).astype(BF16)
    for d in range(1, 8):
        copies.send(("piece", d), piece_out, piece_in.at[q], to_patch(d))
    piece_in[q] = piece_out[...]
    for d in range(1, 8):
        copies.wait(("piece", d), piece_in.at[(q + 8 - d) % 8], to_patch(d))
    for block in range(8):
        pooled_ref[:, block * 128 : block * 128 + 128] = piece_in[block]
    copies.drain()
    assert len(copies.slots) <= SLOTS


def on_device(
    tokens,
    frame_gain,
    qkv_weight,
    out_weight,
    pool_gain,
    latent_gain,
    latents,
    query_weight,
    kv_weight,
    clip_starts,
    valid_frames,
):
    frames_dev, patch_dev, width = tokens.shape
    vmem = pl.BlockSpec(memory_space=pltpu.VMEM)
    smem = pl.BlockSpec(memory_space=pltpu.SMEM)
    temporal_out, pooled = pl.pallas_call(
        kernel,
        out_shape=(
            jax.ShapeDtypeStruct((128, D), BF16),
            jax.ShapeDtypeStruct((128, D), BF16),
        ),
        in_specs=[smem, smem] + [vmem] * 9,
        out_specs=(vmem, vmem),
        scratch_shapes=[
            pltpu.VMEM((4, 32, D), BF16),
            pltpu.VMEM((4, 32, D), BF16),
            pltpu.VMEM((16, 32, D), BF16),
            pltpu.VMEM((8, 4, 192, 128), BF16),
            pltpu.VMEM((8, 16, 64, 128), BF16),
            pltpu.VMEM((8, 16, 144, 128), BF16),
            pltpu.VMEM((2, 4, 64, 256), BF16),
            pltpu.VMEM((2, 4, 64, 256), BF16),
            pltpu.VMEM((2, 4, 16, D), BF16),
            pltpu.VMEM((2, 4, 16, D), BF16),
            pltpu.VMEM((2, 4, 16, D), BF16),
            pltpu.VMEM((64, D), BF16),
            pltpu.VMEM((4, 16, 128), BF16),
            pltpu.VMEM((4, 256, 256), BF16),
            pltpu.VMEM((4, 128, 256), BF16),
            pltpu.VMEM((4, 256, 128), BF16),
            pltpu.VMEM((8, 128), jnp.int32),
            pltpu.VMEM((2, 8, 128), jnp.int32),
            pltpu.VMEM((4, 2, 256, 128), BF16),
            pltpu.VMEM((8, 256, 128), BF16),
            pltpu.VMEM((4, 2, 8, 128), F32),
            pltpu.VMEM((8, 8, 128), F32),
            pltpu.VMEM((2, 64, 128), BF16),
            pltpu.VMEM((2, 64, 128), BF16),
            pltpu.VMEM((8, 128), F32),
            pltpu.VMEM((2, 8, 128), F32),
            pltpu.VMEM((128, 128), BF16),
            pltpu.VMEM((8, 128, 128), BF16),
            pltpu.SemaphoreType.DMA((SLOTS,)),
            pltpu.SemaphoreType.DMA((SLOTS,)),
        ],
        compiler_params=pltpu.CompilerParams(
            collective_id=0, has_side_effects=True, vmem_limit_bytes=48 * 1024 * 1024
        ),
    )(
        clip_starts,
        valid_frames,
        tokens.reshape(frames_dev * patch_dev, width),
        frame_gain.reshape(1, width),
        qkv_weight.T,
        out_weight,
        pool_gain.reshape(1, width),
        latent_gain.reshape(1, width),
        latents,
        query_weight.T,
        kv_weight,
    )
    return (
        temporal_out.reshape(frames_dev, patch_dev, width),
        pooled.reshape(2, 64, width),
    )


def solution(mesh):
    in_specs = (
        P(("dp", "tm"), "patch", None),
        P(),
        P(None, "tm"),
        P("tm", None),
        P(),
        P(),
        P(),
        P(None, "tm"),
        P(None, "tm"),
        P(("dp", "tm")),
        P("dp"),
    )
    out_specs = (P(("dp", "tm"), "patch", None), P(("dp", "tm"), None, None))
    return jax.shard_map(
        on_device, mesh=mesh, in_specs=in_specs, out_specs=out_specs, check_vma=False
    )
```

time: 113 us -> 115 us (1.018)
  the two profiles are of different devices: /device:TPU:33 before, /device:TPU:65 now
where the time goes in v2:
time: 115 us
  Pallas kernels  106 us (92%)
  local copies, waits for them, and re-layouts  7.69 us (7%)
  between operations  1.35 us (1%)
    pallas_call x1, Pallas kernels, on_device(): pl.pallas_call(kernel, out_shape=(jax.ShapeDtypeStruct((128, D), BF16), j...  106 us
    unnamed x22, local copies, waits for them, and re-layouts  7.69 us

profile of v2, /device:TPU:65, one launch (start us, length us, event | category | flops | bytes accessed | tf_op | source)
XLA Modules:
  0.0 114.8 jit_solution(8825121808660582152)
XLA Ops:
  0.6 0.0 copy-start.8
  1.3 0.0 copy-start.7
  1.3 0.0 copy-start.6
  1.3 0.0 copy-start.9
  1.3 0.0 copy-done.8
  1.3 0.6 copy-done.7
  2.0 0.0 copy-done.6
  2.0 0.0 copy-done.9
  2.0 0.0 copy-start
  2.0 1.0 copy-done
  3.0 0.0 copy-start.1
  3.0 0.9 copy-done.1
  4.0 0.0 copy-start.2
  4.0 0.9 copy-done.2
  4.9 0.0 copy-start.3
  4.9 0.9 copy-done.3
  5.8 0.0 copy-start.4
  5.8 0.9 copy-done.4
  6.7 0.0 copy-start.5
  6.7 0.9 copy-done.5
  7.6 105.8 %shard_map.122 = (bf16[128,1024]{1,0:T(8,128)(2,1)S(1)}, bf16[128,1024]{1,0:T(8,128)(2,1)S(1)}) custom-call(s32[2]{0:T(128)S(1)} %copy-done.9, s32[1]{0:T(128)S(6)} %copy.15.valid_ref, bf16[128,1024]{1,0:T(8,128)(2,1)S(1)} %bitcast.11, f32[1,1024]{1,0:T(1,128)S(1)} %bitcast.13, bf16[192,1024]{1,0:T(8,128)(2,1)S(1)} %bitcast.8, ...), custom_call_target="tpu_custom_call" | custom-call | tf_op jit(solution)/shard_map/pallas_call | solution.py:550
  113.4 0.7 copy.16
  114.1 0.7 copy.17
Async XLA Ops:
  0.6 0.7 copy-start.8
  1.3 0.7 copy-start.7
  1.3 0.7 copy-start.6
  1.3 0.7 copy-start.9
  2.0 1.0 copy-start
  3.0 0.9 copy-start.1
  4.0 0.9 copy-start.2
  4.9 0.9 copy-start.3
  5.8 0.9 copy-start.4
  6.7 0.9 copy-start.5

commit v3 on v2

--- a/solution.py
+++ b/solution.py
@@ -14,7 +14,7 @@
 EPS = 1e-05
 NEG = -1e30
 SCALE = HEAD ** (-0.5)
-SLOTS = 160
+SLOTS = 200
 NEAR_FIRST = (1, 3, 2)
 
 
@@ -61,25 +61,35 @@
     def wait(self, name, dst, device):
         self.make(name, dst, dst, device).wait_recv()
 
-    def drain(self):
-        for copy in self.started:
+    def drain(self, count=None):
+        done, self.started = self.started[:count], self.started[len(self.started[:count]) :]
+        for copy in done:
             copy.wait_send()
 
 
 def kernel(
+    starts_hbm,
+    valid_hbm,
+    tokens_hbm,
+    frame_gain_hbm,
+    qkv_hbm,
+    out_w_hbm,
+    pool_gain_hbm,
+    latent_gain_hbm,
+    latents_hbm,
+    query_w_hbm,
+    kv_w_hbm,
+    temporal_ref,
+    pooled_ref,
     starts_ref,
     valid_ref,
     tokens_ref,
     frame_gain_ref,
-    qkv_ref,
-    out_w_ref,
     pool_gain_ref,
     latent_gain_ref,
     latents_ref,
     query_w_ref,
     kv_w_ref,
-    temporal_ref,
-    pooled_ref,
     own_rows,
     rows,
     normed,
@@ -94,7 +104,7 @@
     latn,
     held_queries,
     block_queries,
-    keys,
+    scores_at,
     values,
     start_out,
     start_in,
@@ -108,6 +118,7 @@
     nstat_in,
     piece_out,
     piece_in,
+    load_sem,
     send_sem,
     recv_sem,
 ):
@@ -152,22 +163,61 @@
     for partner in partners:
         pl.semaphore_signal(barrier, inc=1, device_id=partner, device_id_type=MESH)
 
+    eighth = pl.ds(pl.multiple_of(q * 128, 128), 128)
+    loads = [
+        pltpu.make_async_copy(src, dst, load_sem.at[number])
+        for number, (src, dst) in enumerate(
+            [(tokens_hbm, tokens_ref)]
+            + [(qkv_hbm.at[:, pl.ds(b * 128, 128)], wqkv.at[b, g]) for b in range(8)]
+            + [
+                (out_w_hbm.at[:, eighth], wout.at[q, t]),
+                (frame_gain_hbm, frame_gain_ref),
+                (latents_hbm, latents_ref),
+                (latent_gain_hbm, latent_gain_ref),
+                (query_w_hbm, query_w_ref),
+                (kv_w_hbm.at[eighth, :], kv_w_ref),
+                (pool_gain_hbm, pool_gain_ref),
+                (starts_hbm, starts_ref),
+                (valid_hbm, valid_ref),
+            ]
+        )
+    ]
+    for load in loads:
+        load.start()
+
     to_row = lax.broadcasted_iota(jnp.int32, (128, 128), 0)
     from_row = lax.broadcasted_iota(jnp.int32, (128, 128), 1)
-    by_position = jnp.where(from_row == (to_row & 15) * 8 + (to_row >> 4), 1.0, 0.0).astype(BF16)
+    by_position = jnp.where(
+        from_row == (to_row & 15) * 8 + ((to_row >> 4) & 3) * 2 + (to_row >> 6), 1.0, 0.0
+    ).astype(BF16)
+    loads[0].wait()
     for half in range(2):
         cols = slice(half * 512, half * 512 + 512)
-        own_rows[:, :, cols] = dot(by_position, tokens_ref[:, cols]).astype(BF16).reshape(4, 32, 512)
-    for block in range(8):
-        wqkv[block, g] = qkv_ref[:, block * 128 : block * 128 + 128]
+        moved = dot(by_position, tokens_ref[:, cols]).astype(BF16)
+        own_rows[:, :, :, cols] = moved.reshape(2, 4, 16, 512)
+    for load in loads[1:10]:
+        load.wait()
 
     pl.semaphore_wait(barrier, len(partners))
 
     for d in NEAR_FIRST:
         copies.send(f"wqkv_z{d}", wqkv.at[q, g], wqkv.at[q, g], to_z(d))
     for d in NEAR_FIRST:
-        copies.send(f"rows{d}", own_rows.at[at_z(d)], rows.at[g], to_z(d))
-
+        copies.send(f"wout_z{d}", wout.at[q, t], wout.at[q, t], to_z(d))
+    def send_rows(position):
+        for d in NEAR_FIRST:
+            copies.send(
+                ("rows", d, position),
+                own_rows.at[position, at_z(d)],
+                rows.at[position, g],
+                to_z(d),
+            )
+
+    send_rows(0)
+    send_rows(1)
+
+    for load in loads[10:]:
+        load.wait()
     lane = lax.broadcasted_iota(jnp.int32, (8, 128), 1)
     start_out[...] = jnp.where(lane < 64, starts_ref[0], starts_ref[1])
     copies.send("start_after", start_out, start_in.at[0], after)
@@ -175,22 +225,33 @@
 
     frame_gain = frame_gain_ref[...]
 
-    def spread_rows(number, source):
+    def spread_rows(position, number, source):
         shard = y * 4 + source
-        normed[shard] = layer_norm(rows[source].astype(F32), frame_gain).astype(BF16)
+        value = layer_norm(rows[position, source].astype(F32), frame_gain)
+        normed[position, shard] = value.astype(BF16)
+        part = normed.at[position, shard]
         for d in NEAR_FIRST:
-            copies.send(("normed", d, number), normed.at[shard], normed.at[shard], to_y(d))
-
-    rows[g] = own_rows[g]
-    spread_rows(0, g)
-
-    eighth = pl.ds(pl.multiple_of(q * 128, 128), 128)
-    wout[q, t] = out_w_ref[:, eighth]
+            copies.send(("normed", d, position, number), part, part, to_y(d))
+
+    def receive_rows(position):
+        for number, d in ((1, 1), (2, 3), (3, 2)):
+            copies.wait(("rows", d, position), rows.at[position, at_z(-d)], to_z(d))
+            spread_rows(position, number, at_z(-d))
+
+    def receive_normed(position):
+        for number, source in enumerate((0, 1, 3, 2)):
+            for d in NEAR_FIRST:
+                shard = at_y(-d) * 4 + at_z(-source)
+                copies.wait(("normed", d, position, number), normed.at[position, shard], to_y(d))
+
+    for position in range(2):
+        rows[position, g] = own_rows[position, g]
+        spread_rows(position, 0, g)
 
     latn[...] = layer_norm(latents_ref[...].astype(F32), latent_gain_ref[...]).astype(BF16)
     queries = dot_nt(query_w_ref[...], latn[...])
     held_queries[...] = jnp.concatenate([queries, queries], axis=1).astype(BF16).reshape(4, 16, 128)
-    wkv[q, t, 0:128, :] = jnp.transpose(kv_w_ref[eighth, :].astype(F32)).astype(BF16)
+    wkv[q, t, 0:128, :] = jnp.transpose(kv_w_ref[...].astype(F32)).astype(BF16)
     wkv[q, t, 128:144, :] = held_queries[q // 2]
 
     def unit_start(name, buf, part):
@@ -237,12 +298,7 @@
         )
 
     out_units = [y_unit("wout", wout, d) for d in (0, 1, 3, 2)]
-    kv_units = [y_unit("wkv", wkv, d) for d in (0, 1, 3, 2)]
     qkv_units = [qkv_unit(d) for d in NEAR_FIRST]
-
-    def over_z(name, buf):
-        for d in NEAR_FIRST:
-            copies.send(f"{name}_z{d}", buf.at[q, t], buf.at[q, t], to_z(d))
 
     def over_y(name, buf):
         for d in NEAR_FIRST:
@@ -259,30 +315,28 @@
     for d, unit in zip(NEAR_FIRST, qkv_units):
         copies.wait(f"wqkv_z{d}", wqkv.at[q, at_z(-d)], to_z(d))
         unit_start(*unit[:3])
-    for number, d in ((1, 1), (2, 3)):
-        copies.wait(f"rows{d}", rows.at[at_z(-d)], to_z(d))
-        spread_rows(number, at_z(-d))
+    over_y("wout", wout)
+    unit_start(*out_units[0][:3])
+    receive_rows(0)
     for unit in qkv_units:
         unit_relay(*unit)
-    copies.wait("rows2", rows.at[at_z(-2)], to_z(2))
-    spread_rows(3, at_z(-2))
-    over_z("wout", wout)
-    over_z("wkv", wkv)
+    for d in NEAR_FIRST:
+        copies.send(f"wkv_z{d}", wkv.at[q, t], wkv.at[q, t], to_z(d))
+    receive_rows(1)
     for unit in qkv_units:
         unit_far(*unit)
-    for number, source in enumerate((0, 1, 3, 2)):
-        for d in NEAR_FIRST:
-            shard = at_y(-d) * 4 + at_z(-source)
-            copies.wait(("normed", d, number), normed.at[shard], to_y(d))
+    from_y("wout", wout, out_units)
+    receive_normed(0)
     for unit in qkv_units:
         unit_end(*unit[:3])
+    early = len(copies.started)
 
     valid = valid_ref[0]
     key_live = lax.broadcasted_iota(jnp.int32, (256, 256), 1) < valid
     first_head = lax.broadcasted_iota(jnp.int32, (256, 128), 1) < 64
 
     def attend(position):
-        here = normed[:, position * 16 : position * 16 + 16, :].reshape(256, D)
+        here = normed[position].reshape(256, D)
         for pair in range(2):
             blocks = []
             for block in range(8):
@@ -320,7 +374,7 @@
                 [wout[2 * block].reshape(D, 128), wout[2 * block + 1].reshape(D, 128)], axis=1
             )
             cols = slice(block * 256, block * 256 + 256)
-            tokens = rows[:, position * 16 : position * 16 + 16, cols]
+            tokens = rows[position, :, :, cols]
             total = tokens.astype(F32).reshape(64, 256) + dot(attended, weight)
             summed[position, :, :, cols] = total.astype(BF16).reshape(4, 16, 256)
         for d in NEAR_FIRST:
@@ -330,56 +384,66 @@
         back[position, g] = summed[position, g]
 
     attend(0)
-    over_y("wout", wout)
-    unit_start(*out_units[0][:3])
-    attend(1)
-    over_y("wkv", wkv)
-    unit_start(*kv_units[0][:3])
-    from_y("wout", wout, out_units)
     for unit in out_units:
         unit_relay(*unit)
-    from_y("wkv", wkv, kv_units)
+    over_y("wkv", wkv)
+    receive_normed(1)
+    attend(1)
     for unit in out_units:
         unit_far(*unit)
+    for d in NEAR_FIRST:
+        copies.wait(("wkv", "y", d), wkv.at[q, pl.ds(at_y(-d) * 4, 4)], to_y(d))
+    for k in NEAR_FIRST:
+        there = (x + k) % 4
+        part = wkv.at[q, pl.ds(there * 4, 4)]
+        copies.send(("wkv", "x", k), part, part, to_x(k))
+    own_heads = pl.ds(x * 4, 4)
+    copies.send(("wkv", "core", 0), wkv.at[q, own_heads], wkv.at[q, own_heads], sibling)
     for unit in out_units:
         unit_end(*unit[:3])
     project(0)
     project(1)
 
-    for unit in kv_units:
-        unit_relay(*unit)
-    for unit in kv_units:
-        unit_far(*unit)
+    for k in NEAR_FIRST:
+        part = wkv.at[at_x(-k), own_heads]
+        copies.wait(("wkv", "x", k), part, to_x(k))
+        copies.send(("wkv", "core", k), part, part, sibling)
+    copies.drain(early)
     copies.wait("start_after", start_in.at[0], after)
     copies.wait("start_before", start_in.at[1], before)
 
     pool_gain = pool_gain_ref[...]
 
-    def pool_norm(position, source):
+    def pool_norm(position, number, source):
         value = layer_norm(back[position, source].astype(F32), pool_gain)
-        pooled[position, source] = value.astype(BF16)
+        pooled[x, position, source] = value.astype(BF16)
+        part = pooled.at[x, position, source]
+        for k in NEAR_FIRST:
+            copies.send(("pooled", k, position, number), part, part, to_x(k))
+
+    pool_norm(0, 0, g)
+    pool_norm(1, 0, g)
+    for d in (0,) + NEAR_FIRST:
+        other = ((x - d + 4) % 4) * 2 + 1 - c
+        copies.wait(("wkv", "core", d), wkv.at[other, own_heads], sibling)
+
+    wide_lane = lax.broadcasted_iota(jnp.int32, (64, 256), 1)
+    for head in range(4):
+        parts = [wkv[2 * block, 4 * x + head, 128:144, :] for block in range(4)]
+        query = jnp.concatenate(parts, axis=0)
+        query = jnp.concatenate([query, query], axis=1)
+        block_queries[head * 64 : head * 64 + 64, :] = jnp.where(
+            (wide_lane >> 6) == head, query, jnp.zeros_like(query)
+        )
 
     for position in range(2):
-        pool_norm(position, g)
-        for d in NEAR_FIRST:
+        for number, d in ((1, 1), (2, 3), (3, 2)):
             copies.wait(("back", d, position), back.at[position, at_z(-d)], to_z(d))
-            pool_norm(position, at_z(-d))
-    for unit in kv_units:
-        unit_end(*unit[:3])
-
-    wide_lane = lax.broadcasted_iota(jnp.int32, (64, 256), 1)
-    for quad in range(4):
-        for head in range(4):
-            parts = [wkv[2 * block, 4 * quad + head, 128:144, :] for block in range(4)]
-            query = jnp.concatenate(parts, axis=0)
-            query = jnp.concatenate([query, query], axis=1)
-            block_queries[quad, head * 64 : head * 64 + 64, :] = jnp.where(
-                (wide_lane >> 6) == head, query, jnp.zeros_like(query)
-            )
+            pool_norm(position, number, at_z(-d))
 
     far_starts = jnp.where(lane < 64, start_in[1], start_in[0])[0:1]
     own_starts = start_out[0:1, :]
-    frame = t * 16 + (lax.broadcasted_iota(jnp.int32, (128, 128), 0) & 15)
+    frame = t * 16 + (lax.broadcasted_iota(jnp.int32, (128, 256), 0) & 15)
     in_lane = lax.broadcasted_iota(jnp.int32, (1, 128), 1)
 
     def live_of(starts, second):
@@ -393,53 +457,51 @@
         live_of(far_starts, False),
         live_of(far_starts, True),
     ]
-    live = [jnp.concatenate([mask, mask], axis=1) for mask in live]
     pair_lane = lax.broadcasted_iota(jnp.int32, (64, 128), 1)
-    rows_now = pooled[...].reshape(128, D)
-
-    def kv_project(quad):
-        key_blocks, value_blocks = [], []
-        for block in range(8):
-            four = wkv[block, pl.ds(quad * 4, 4)]
-            key_blocks.append(four[:, 0:64, :].reshape(256, 128))
-            value_blocks.append(four[:, 64:128, :].reshape(256, 128))
-        keys[quad] = dot_nt(rows_now, jnp.concatenate(key_blocks, axis=1)).astype(BF16)
-        values[quad] = dot_nt(jnp.concatenate(value_blocks, axis=1), rows_now).astype(BF16)
-
-    def pool_quad(quad):
-        scores = dot(keys[quad], block_queries[quad]) * SCALE
-        value = values[quad]
-        for clip in range(4):
-            top = jnp.max(jnp.where(live[clip], scores, NEG), axis=0, keepdims=True)
-            weights = jnp.where(live[clip], jnp.exp(scores - top), 0.0)
-            total = jnp.sum(weights, axis=0, keepdims=True)
-            mix = dot(value, weights.astype(BF16))
-            for pair in range(2):
-                cols = slice(pair * 128, pair * 128 + 128)
-                even = mix[pair * 128 : pair * 128 + 64, cols]
-                odd = mix[pair * 128 + 64 : pair * 128 + 128, cols]
-                part_out[quad, pair, clip * 64 : clip * 64 + 64, :] = jnp.where(
-                    pair_lane < 64, even, odd
-                ).astype(BF16)
-                stat_out[quad, pair, clip : clip + 1, :] = top[:, cols]
-                stat_out[quad, pair, 4 + clip : 5 + clip, :] = total[:, cols]
-
-    def send_part(name, quad, core):
-        device = {"patch": quad * 2 + core}
-        copies.send(("part", name), part_out.at[quad, core], part_in.at[q], device)
-        copies.send(("stat", name), stat_out.at[quad, core], stat_in.at[q], device)
-
-    order = [(x + k) % 4 for k in (2, 1, 3, 0)]
-    kv_project(order[0])
-    for number, quad in enumerate(order):
-        if number < 3:
-            kv_project(order[number + 1])
-        pool_quad(quad)
-        if number < 3:
-            send_part(("same", number), quad, c)
-        send_part(("cross", number), quad, 1 - c)
-    part_in[q] = part_out[x, c]
-    stat_in[q] = stat_out[x, c]
+    key_blocks, value_blocks = [], []
+    for block in range(8):
+        four = wkv[block, own_heads]
+        key_blocks.append(four[:, 0:64, :].reshape(256, 128))
+        value_blocks.append(four[:, 64:128, :].reshape(256, 128))
+    key_weight = jnp.concatenate(key_blocks, axis=1)
+    value_weight = jnp.concatenate(value_blocks, axis=1)
+
+    def pool_project(place, source):
+        here = pooled[source].reshape(128, D)
+        key = dot_nt(here, key_weight).astype(BF16)
+        scores_at[place] = dot(key, block_queries[...]) * SCALE
+        values[:, place * 128 : place * 128 + 128] = dot_nt(value_weight, here).astype(BF16)
+
+    pool_project(0, x)
+    for place, k in ((1, 1), (2, 3), (3, 2)):
+        source = (x - k + 4) % 4
+        for position in range(2):
+            for number, d in enumerate((0, 1, 3, 2)):
+                part = pooled.at[source, position, at_z(-d)]
+                copies.wait(("pooled", k, position, number), part, to_x(k))
+        pool_project(place, source)
+
+    for clip in range(4):
+        top = jnp.full((1, 256), NEG, F32)
+        for place in range(4):
+            kept = jnp.where(live[clip], scores_at[place], NEG)
+            top = jnp.maximum(top, jnp.max(kept, axis=0, keepdims=True))
+        weights = [
+            jnp.where(live[clip], jnp.exp(scores_at[place] - top), 0.0) for place in range(4)
+        ]
+        total = sum(jnp.sum(weight, axis=0, keepdims=True) for weight in weights)
+        mix = dot(values[...], jnp.concatenate([w.astype(BF16) for w in weights], axis=0))
+        for pair in range(2):
+            cols = slice(pair * 128, pair * 128 + 128)
+            even = mix[pair * 128 : pair * 128 + 64, cols]
+            odd = mix[pair * 128 + 64 : pair * 128 + 128, cols]
+            part_out[pair, clip * 64 : clip * 64 + 64, :] = jnp.where(
+                pair_lane < 64, even, odd
+            ).astype(BF16)
+            stat_out[pair, clip : clip + 1, :] = top[:, cols]
+            stat_out[pair, 4 + clip : 5 + clip, :] = total[:, cols]
+    copies.send("part", part_out.at[1 - c], part_in, sibling)
+    copies.send("stat", stat_out.at[1 - c], stat_in, sibling)
 
     key_blocks, value_blocks = [], []
     for block in range(8):
@@ -449,7 +511,7 @@
     self_key = dot_nt(latn[...], jnp.concatenate(key_blocks, axis=1)).astype(BF16)
     self_value = dot_nt(jnp.concatenate(value_blocks, axis=1), latn[...]).astype(BF16)
     pair_queries = jnp.where(
-        c == 0, block_queries[x, 0:128, 0:128], block_queries[x, 128:256, 128:256]
+        c == 0, block_queries[0:128, 0:128], block_queries[128:256, 128:256]
     )
     self_scores = dot(self_key, pair_queries) * SCALE
     self_top = jnp.max(self_scores, axis=0, keepdims=True)
@@ -462,14 +524,9 @@
         cols = slice(half * 512, half * 512 + 512)
         temporal_ref[:, cols] = dot(by_frame, held[:, cols]).astype(BF16)
 
-    for number, k in enumerate((2, 1, 3, 0)):
-        source = ((x + 4 - k) % 4) * 2
-        if number < 3:
-            copies.wait(("part", ("same", number)), part_in.at[source + c], to_x(k))
-            copies.wait(("stat", ("same", number)), stat_in.at[source + c], to_x(k))
-        copies.wait(("part", ("cross", number)), part_in.at[source + 1 - c], sibling)
-        copies.wait(("stat", ("cross", number)), stat_in.at[source + 1 - c], sibling)
-    stats = [stat_in[source] for source in range(8)]
+    copies.wait("part", part_in, sibling)
+    copies.wait("stat", stat_in, sibling)
+    stats = [stat_out[c], stat_in[...]]
     highest = stats[0][0:4]
     for stat in stats[1:]:
         highest = jnp.maximum(highest, stat[0:4])
@@ -482,9 +539,9 @@
 
     def gathered(clip):
         mix = jnp.zeros((64, 128), F32)
-        for source in range(8):
-            part = part_in[source, clip * 64 : clip * 64 + 64, :].astype(F32)
-            mix += part * factors[source][clip : clip + 1]
+        span = slice(clip * 64, clip * 64 + 64)
+        for part, factor in zip((part_out[c, span, :], part_in[span, :]), factors):
+            mix += part.astype(F32) * factor[clip : clip + 1]
         return mix
 
     near_out[0] = gathered(2).astype(BF16)
@@ -546,19 +603,27 @@
 ):
     frames_dev, patch_dev, width = tokens.shape
     vmem = pl.BlockSpec(memory_space=pltpu.VMEM)
-    smem = pl.BlockSpec(memory_space=pltpu.SMEM)
     temporal_out, pooled = pl.pallas_call(
         kernel,
         out_shape=(
             jax.ShapeDtypeStruct((128, D), BF16),
             jax.ShapeDtypeStruct((128, D), BF16),
         ),
-        in_specs=[smem, smem] + [vmem] * 9,
+        in_specs=[pl.BlockSpec(memory_space=pl.ANY)] * 11,
         out_specs=(vmem, vmem),
         scratch_shapes=[
-            pltpu.VMEM((4, 32, D), BF16),
-            pltpu.VMEM((4, 32, D), BF16),
-            pltpu.VMEM((16, 32, D), BF16),
+            pltpu.SMEM((2,), jnp.int32),
+            pltpu.SMEM((1,), jnp.int32),
+            pltpu.VMEM((128, D), BF16),
+            pltpu.VMEM((1, D), F32),
+            pltpu.VMEM((1, D), F32),
+            pltpu.VMEM((1, D), F32),
+            pltpu.VMEM((64, D), BF16),
+            pltpu.VMEM((64, D), BF16),
+            pltpu.VMEM((128, 128), BF16),
+            pltpu.VMEM((2, 4, 16, D), BF16),
+            pltpu.VMEM((2, 4, 16, D), BF16),
+            pltpu.VMEM((2, 16, 16, D), BF16),
             pltpu.VMEM((8, 4, 192, 128), BF16),
             pltpu.VMEM((8, 16, 64, 128), BF16),
             pltpu.VMEM((8, 16, 144, 128), BF16),
@@ -566,29 +631,30 @@
             pltpu.VMEM((2, 4, 64, 256), BF16),
             pltpu.VMEM((2, 4, 16, D), BF16),
             pltpu.VMEM((2, 4, 16, D), BF16),
-            pltpu.VMEM((2, 4, 16, D), BF16),
+            pltpu.VMEM((4, 2, 4, 16, D), BF16),
             pltpu.VMEM((64, D), BF16),
             pltpu.VMEM((4, 16, 128), BF16),
-            pltpu.VMEM((4, 256, 256), BF16),
-            pltpu.VMEM((4, 128, 256), BF16),
-            pltpu.VMEM((4, 256, 128), BF16),
+            pltpu.VMEM((256, 256), BF16),
+            pltpu.VMEM((4, 128, 256), F32),
+            pltpu.VMEM((256, 512), BF16),
             pltpu.VMEM((8, 128), jnp.int32),
             pltpu.VMEM((2, 8, 128), jnp.int32),
-            pltpu.VMEM((4, 2, 256, 128), BF16),
-            pltpu.VMEM((8, 256, 128), BF16),
-            pltpu.VMEM((4, 2, 8, 128), F32),
-            pltpu.VMEM((8, 8, 128), F32),
+            pltpu.VMEM((2, 256, 128), BF16),
+            pltpu.VMEM((256, 128), BF16),
+            pltpu.VMEM((2, 8, 128), F32),
+            pltpu.VMEM((8, 128), F32),
             pltpu.VMEM((2, 64, 128), BF16),
             pltpu.VMEM((2, 64, 128), BF16),
             pltpu.VMEM((8, 128), F32),
             pltpu.VMEM((2, 8, 128), F32),
             pltpu.VMEM((128, 128), BF16),
             pltpu.VMEM((8, 128, 128), BF16),
+            pltpu.SemaphoreType.DMA((18,)),
             pltpu.SemaphoreType.DMA((SLOTS,)),
             pltpu.SemaphoreType.DMA((SLOTS,)),
         ],
         compiler_params=pltpu.CompilerParams(
-            collective_id=0, has_side_effects=True, vmem_limit_bytes=48 * 1024 * 1024
+            collective_id=0, has_side_effects=True, vmem_limit_bytes=62 * 1024 * 1024
         ),
     )(
         clip_starts,

time: 115 us -> 105 us (0.913)
  the two profiles are of different devices: /device:TPU:65 before, /device:TPU:33 now
where the time goes in v3:
time: 105 us
  Pallas kernels  101 us (96%)
  local copies, waits for them, and re-layouts  2.42 us (2%)
  between operations  1.3 us (1%)
    pallas_call x1, Pallas kernels, on_device(): pl.pallas_call(kernel, out_shape=(jax.ShapeDtypeStruct((128, D), BF16), j...  101 us
    unnamed x4, local copies, waits for them, and re-layouts  2.42 us

profile of v3, /device:TPU:33, one launch (start us, length us, event | category | flops | bytes accessed | tf_op | source)
XLA Modules:
  0.0 105.2 jit_solution(8588387821510007816)
XLA Ops:
  1.3 101.5 %shard_map.122 = (bf16[128,1024]{1,0:T(8,128)(2,1)}, bf16[128,1024]{1,0:T(8,128)(2,1)}) custom-call(s32[2]{0:T(128)} %starts_hbm.1, s32[1]{0:T(128)S(6)} %copy.15.valid_hbm, bf16[128,1024]{1,0:T(8,128)(2,1)} %bitcast.11, f32[1,1024]{1,0:T(1,128)} %bitcast.13, bf16[192,1024]{1,0:T(8,128)(2,1)} %bitcast.8, bf16[64,1024]{1,0:T(8,128)(2,1)} %out_w_hbm.1, ...), custom_call_target="tpu_custom_call" | custom-call | tf_op jit(solution)/shard_map/pallas_call | solution.py:606
  102.8 0.0 copy-start
  102.8 1.7 %copy.16 = bf16[16,8,1024]{2,1,0:T(8,128)(2,1)} copy(bf16[16,8,1024]{2,1,0:T(8,128)(2,1)} %bitcast.10) | data formatting | bytes 524288
  104.5 0.0 copy-done
  104.5 0.7 copy.17
Async XLA Ops:
  102.8 1.7 %copy-start = (bf16[128,1024]{1,0:T(8,128)(2,1)S(1)}, bf16[128,1024]{1,0:T(8,128)(2,1)}, u32[]{:S(2)}) copy-start(bf16[128,1024]{1,0:T(8,128)(2,1)} %get-tuple-element.5) | copy-start | bytes 786436

commit v4 on v3

--- a/solution.py
+++ b/solution.py
@@ -14,7 +14,7 @@
 EPS = 1e-05
 NEG = -1e30
 SCALE = HEAD ** (-0.5)
-SLOTS = 200
+SLOTS = 144
 NEAR_FIRST = (1, 3, 2)
 
 
@@ -153,24 +153,14 @@
     after = {"tm": (t + 1) % 16}
     before = {"tm": (t + 15) % 16}
 
-    barrier = pltpu.get_barrier_semaphore()
-    partners = (
-        [to_z(d) for d in (1, 2, 3)]
-        + [to_y(d) for d in (1, 2, 3)]
-        + [to_patch(d) for d in range(1, 8)]
-        + [after, before]
-    )
-    for partner in partners:
-        pl.semaphore_signal(barrier, inc=1, device_id=partner, device_id_type=MESH)
-
     eighth = pl.ds(pl.multiple_of(q * 128, 128), 128)
     loads = [
         pltpu.make_async_copy(src, dst, load_sem.at[number])
         for number, (src, dst) in enumerate(
             [(tokens_hbm, tokens_ref)]
-            + [(qkv_hbm.at[:, pl.ds(b * 128, 128)], wqkv.at[b, g]) for b in range(8)]
+            + [(qkv_hbm.at[:, pl.ds(b * 128, 128)], wqkv.at[b, 0]) for b in range(8)]
             + [
-                (out_w_hbm.at[:, eighth], wout.at[q, t]),
+                (out_w_hbm.at[:, eighth], wout.at[q, 0, 0]),
                 (frame_gain_hbm, frame_gain_ref),
                 (latents_hbm, latents_ref),
                 (latent_gain_hbm, latent_gain_ref),
@@ -185,6 +175,16 @@
     for load in loads:
         load.start()
 
+    barrier = pltpu.get_barrier_semaphore()
+    partners = (
+        [to_z(d) for d in (1, 2, 3)]
+        + [to_y(d) for d in (1, 2, 3)]
+        + [to_patch(d) for d in range(1, 8)]
+        + [after, before]
+    )
+    for partner in partners:
+        pl.semaphore_signal(barrier, inc=1, device_id=partner, device_id_type=MESH)
+
     to_row = lax.broadcasted_iota(jnp.int32, (128, 128), 0)
     from_row = lax.broadcasted_iota(jnp.int32, (128, 128), 1)
     by_position = jnp.where(
@@ -201,9 +201,9 @@
     pl.semaphore_wait(barrier, len(partners))
 
     for d in NEAR_FIRST:
-        copies.send(f"wqkv_z{d}", wqkv.at[q, g], wqkv.at[q, g], to_z(d))
-    for d in NEAR_FIRST:
-        copies.send(f"wout_z{d}", wout.at[q, t], wout.at[q, t], to_z(d))
+        copies.send(f"wqkv_z{d}", wqkv.at[q, 0], wqkv.at[q, d], to_z(d))
+    for d in NEAR_FIRST:
+        copies.send(f"wout_z{d}", wout.at[q, 0, 0], wout.at[q, 0, d], to_z(d))
     def send_rows(position):
         for d in NEAR_FIRST:
             copies.send(
@@ -277,58 +277,39 @@
             other = ((x + d + 4) % 4) * 2 + 1 - c
             copies.wait((name, "core", number), part(buf, other), sibling)
 
-    def qkv_unit(d):
-        shard = at_z(-d)
-        return (
-            ("wqkv", d),
-            wqkv,
-            lambda buf, at: buf.at[at, shard],
-            lambda buf, at: buf.at[at, shard, pl.ds(0, 96)],
-            lambda buf, at: buf.at[at, shard, pl.ds(96, 96)],
-        )
-
-    def y_unit(name, buf, d):
-        first = at_y(-d) * 4
-        return (
-            (name, d),
-            buf,
-            lambda buf, at: buf.at[at, pl.ds(first, 4)],
-            lambda buf, at: buf.at[at, pl.ds(first, 2)],
-            lambda buf, at: buf.at[at, pl.ds(first + 2, 2)],
-        )
-
-    out_units = [y_unit("wout", wout, d) for d in (0, 1, 3, 2)]
-    qkv_units = [qkv_unit(d) for d in NEAR_FIRST]
-
-    def over_y(name, buf):
-        for d in NEAR_FIRST:
-            copies.wait(f"{name}_z{d}", buf.at[q, y * 4 + at_z(-d)], to_z(d))
-        part = buf.at[q, pl.ds(y * 4, 4)]
-        for d in NEAR_FIRST:
-            copies.send((name, "y", d), part, part, to_y(d))
-
-    def from_y(name, buf, units):
-        for d, unit in zip(NEAR_FIRST, units[1:]):
-            copies.wait((name, "y", d), buf.at[q, pl.ds(at_y(-d) * 4, 4)], to_y(d))
-            unit_start(*unit[:3])
-
-    for d, unit in zip(NEAR_FIRST, qkv_units):
-        copies.wait(f"wqkv_z{d}", wqkv.at[q, at_z(-d)], to_z(d))
-        unit_start(*unit[:3])
-    over_y("wout", wout)
-    unit_start(*out_units[0][:3])
+    qkv_unit = (
+        "wqkv",
+        wqkv,
+        lambda buf, at: buf.at[at, pl.ds(1, 3)],
+        lambda buf, at: buf.at[at, pl.ds(1, 3), pl.ds(0, 96)],
+        lambda buf, at: buf.at[at, pl.ds(1, 3), pl.ds(96, 96)],
+    )
+    out_unit = (
+        "wout",
+        wout,
+        lambda buf, at: buf.at[at],
+        lambda buf, at: buf.at[at, pl.ds(0, 2)],
+        lambda buf, at: buf.at[at, pl.ds(2, 2)],
+    )
+
+    for d in NEAR_FIRST:
+        copies.wait(f"wqkv_z{d}", wqkv.at[q, d], to_z(d))
+    unit_start(*qkv_unit[:3])
+    for d in NEAR_FIRST:
+        copies.wait(f"wout_z{d}", wout.at[q, 0, d], to_z(d))
+    for d in NEAR_FIRST:
+        copies.send(f"wout_y{d}", wout.at[q, 0], wout.at[q, d], to_y(d))
     receive_rows(0)
-    for unit in qkv_units:
-        unit_relay(*unit)
+    unit_relay(*qkv_unit)
     for d in NEAR_FIRST:
         copies.send(f"wkv_z{d}", wkv.at[q, t], wkv.at[q, t], to_z(d))
+    for d in NEAR_FIRST:
+        copies.wait(f"wout_y{d}", wout.at[q, d], to_y(d))
+    unit_start(*out_unit[:3])
     receive_rows(1)
-    for unit in qkv_units:
-        unit_far(*unit)
-    from_y("wout", wout, out_units)
+    unit_far(*qkv_unit)
     receive_normed(0)
-    for unit in qkv_units:
-        unit_end(*unit[:3])
+    unit_end(*qkv_unit[:3])
     early = len(copies.started)
 
     valid = valid_ref[0]
@@ -361,13 +342,13 @@
             att_out[position, :, :, pair * 128 : pair * 128 + 128] = result.reshape(4, 64, 128)
         for d in NEAR_FIRST:
             copies.send(
-                ("att", d, position), att_out.at[position, at_y(d)], att_in.at[position, y], to_y(d)
+                ("att", d, position), att_out.at[position, at_y(d)], att_in.at[position, d], to_y(d)
             )
-        att_in[position, y] = att_out[position, y]
+        att_in[position, 0] = att_out[position, y]
 
     def project(position):
         for d in NEAR_FIRST:
-            copies.wait(("att", d, position), att_in.at[position, at_y(-d)], to_y(d))
+            copies.wait(("att", d, position), att_in.at[position, d], to_y(d))
         attended = jnp.concatenate([att_in[position, source] for source in range(4)], axis=1)
         for block in range(4):
             weight = jnp.concatenate(
@@ -384,13 +365,15 @@
         back[position, g] = summed[position, g]
 
     attend(0)
-    for unit in out_units:
-        unit_relay(*unit)
-    over_y("wkv", wkv)
+    unit_relay(*out_unit)
+    for d in NEAR_FIRST:
+        copies.wait(f"wkv_z{d}", wkv.at[q, y * 4 + at_z(-d)], to_z(d))
+    part = wkv.at[q, pl.ds(y * 4, 4)]
+    for d in NEAR_FIRST:
+        copies.send(("wkv", "y", d), part, part, to_y(d))
     receive_normed(1)
     attend(1)
-    for unit in out_units:
-        unit_far(*unit)
+    unit_far(*out_unit)
     for d in NEAR_FIRST:
         copies.wait(("wkv", "y", d), wkv.at[q, pl.ds(at_y(-d) * 4, 4)], to_y(d))
     for k in NEAR_FIRST:
@@ -399,8 +382,7 @@
         copies.send(("wkv", "x", k), part, part, to_x(k))
     own_heads = pl.ds(x * 4, 4)
     copies.send(("wkv", "core", 0), wkv.at[q, own_heads], wkv.at[q, own_heads], sibling)
-    for unit in out_units:
-        unit_end(*unit[:3])
+    unit_end(*out_unit[:3])
     project(0)
     project(1)
 
@@ -420,6 +402,11 @@
         part = pooled.at[x, position, source]
         for k in NEAR_FIRST:
             copies.send(("pooled", k, position, number), part, part, to_x(k))
+
+    def receive_back(position):
+        for number, d in ((1, 1), (2, 3), (3, 2)):
+            copies.wait(("back", d, position), back.at[position, at_z(-d)], to_z(d))
+            pool_norm(position, number, at_z(-d))
 
     pool_norm(0, 0, g)
     pool_norm(1, 0, g)
@@ -436,10 +423,21 @@
             (wide_lane >> 6) == head, query, jnp.zeros_like(query)
         )
 
+    key_blocks, value_blocks = [], []
+    for block in range(8):
+        two = wkv[block, pl.ds(q * 2, 2)]
+        key_blocks.append(two[:, 0:64, :].reshape(128, 128))
+        value_blocks.append(two[:, 64:128, :].reshape(128, 128))
+    self_key = dot_nt(latn[...], jnp.concatenate(key_blocks, axis=1)).astype(BF16)
+    self_value = dot_nt(jnp.concatenate(value_blocks, axis=1), latn[...]).astype(BF16)
+    pair_queries = jnp.where(
+        c == 0, block_queries[0:128, 0:128], block_queries[128:256, 128:256]
+    )
+    self_scores = dot(self_key, pair_queries) * SCALE
+    self_top = jnp.max(self_scores, axis=0, keepdims=True)
+
     for position in range(2):
-        for number, d in ((1, 1), (2, 3), (3, 2)):
-            copies.wait(("back", d, position), back.at[position, at_z(-d)], to_z(d))
-            pool_norm(position, number, at_z(-d))
+        receive_back(position)
 
     far_starts = jnp.where(lane < 64, start_in[1], start_in[0])[0:1]
     own_starts = start_out[0:1, :]
@@ -473,6 +471,14 @@
         values[:, place * 128 : place * 128 + 128] = dot_nt(value_weight, here).astype(BF16)
 
     pool_project(0, x)
+
+    by_frame = jnp.where(
+        from_row == (to_row & 1) * 64 + ((to_row & 7) >> 1) * 16 + (to_row >> 3), 1.0, 0.0
+    ).astype(BF16)
+    held = back[...].reshape(128, D)
+    for half in range(2):
+        cols = slice(half * 512, half * 512 + 512)
+        temporal_ref[:, cols] = dot(by_frame, held[:, cols]).astype(BF16)
     for place, k in ((1, 1), (2, 3), (3, 2)):
         source = (x - k + 4) % 4
         for position in range(2):
@@ -502,27 +508,6 @@
             stat_out[pair, 4 + clip : 5 + clip, :] = total[:, cols]
     copies.send("part", part_out.at[1 - c], part_in, sibling)
     copies.send("stat", stat_out.at[1 - c], stat_in, sibling)
-
-    key_blocks, value_blocks = [], []
-    for block in range(8):
-        two = wkv[block, pl.ds(q * 2, 2)]
-        key_blocks.append(two[:, 0:64, :].reshape(128, 128))
-        value_blocks.append(two[:, 64:128, :].reshape(128, 128))
-    self_key = dot_nt(latn[...], jnp.concatenate(key_blocks, axis=1)).astype(BF16)
-    self_value = dot_nt(jnp.concatenate(value_blocks, axis=1), latn[...]).astype(BF16)
-    pair_queries = jnp.where(
-        c == 0, block_queries[0:128, 0:128], block_queries[128:256, 128:256]
-    )
-    self_scores = dot(self_key, pair_queries) * SCALE
-    self_top = jnp.max(self_scores, axis=0, keepdims=True)
-
-    by_frame = jnp.where(
-        from_row == (to_row & 1) * 64 + ((to_row & 7) >> 1) * 16 + (to_row >> 3), 1.0, 0.0
-    ).astype(BF16)
-    held = back[...].reshape(128, D)
-    for half in range(2):
-        cols = slice(half * 512, half * 512 + 512)
-        temporal_ref[:, cols] = dot(by_frame, held[:, cols]).astype(BF16)
 
     copies.wait("part", part_in, sibling)
     copies.wait("stat", stat_in, sibling)
@@ -625,7 +610,7 @@
             pltpu.VMEM((2, 4, 16, D), BF16),
             pltpu.VMEM((2, 16, 16, D), BF16),
             pltpu.VMEM((8, 4, 192, 128), BF16),
-            pltpu.VMEM((8, 16, 64, 128), BF16),
+            pltpu.VMEM((8, 4, 4, 64, 128), BF16),
             pltpu.VMEM((8, 16, 144, 128), BF16),
             pltpu.VMEM((2, 4, 64, 256), BF16),
             pltpu.VMEM((2, 4, 64, 256), BF16),

time: 105 us -> 104 us (level)
  the two profiles are of different devices: /device:TPU:33 before, /device:TPU:45 now
where the time goes in v4:
time: 104 us
  Pallas kernels  100 us (96%)
  local copies, waits for them, and re-layouts  2.42 us (2%)
  between operations  1.3 us (1%)
    pallas_call x1, Pallas kernels, on_device(): pl.pallas_call(kernel, out_shape=(jax.ShapeDtypeStruct((128, D), BF16), j...  100 us
    unnamed x4, local copies, waits for them, and re-layouts  2.42 us

profile of v4, /device:TPU:45, one launch (start us, length us, event | category | flops | bytes accessed | tf_op | source)
XLA Modules:
  0.0 104.2 jit_solution(14154776087308634788)
XLA Ops:
  1.3 100.5 %shard_map.122 = (bf16[128,1024]{1,0:T(8,128)(2,1)}, bf16[128,1024]{1,0:T(8,128)(2,1)}) custom-call(s32[2]{0:T(128)} %starts_hbm.1, s32[1]{0:T(128)S(6)} %copy.15.valid_hbm, bf16[128,1024]{1,0:T(8,128)(2,1)} %bitcast.11, f32[1,1024]{1,0:T(1,128)} %bitcast.13, bf16[192,1024]{1,0:T(8,128)(2,1)} %bitcast.8, bf16[64,1024]{1,0:T(8,128)(2,1)} %out_w_hbm.1, ...), custom_call_target="tpu_custom_call" | custom-call | tf_op jit(solution)/shard_map/pallas_call | solution.py:591
  101.8 0.0 copy-start
  101.8 1.7 %copy.16 = bf16[16,8,1024]{2,1,0:T(8,128)(2,1)} copy(bf16[16,8,1024]{2,1,0:T(8,128)(2,1)} %bitcast.10) | data formatting | bytes 524288
  103.5 0.0 copy-done
  103.5 0.7 copy.17
Async XLA Ops:
  101.8 1.7 %copy-start = (bf16[128,1024]{1,0:T(8,128)(2,1)S(1)}, bf16[128,1024]{1,0:T(8,128)(2,1)}, u32[]{:S(2)}) copy-start(bf16[128,1024]{1,0:T(8,128)(2,1)} %get-tuple-element.5) | copy-start | bytes 786436

commit v5 on v4

--- a/solution.py
+++ b/solution.py
@@ -14,7 +14,7 @@
 EPS = 1e-05
 NEG = -1e30
 SCALE = HEAD ** (-0.5)
-SLOTS = 144
+SLOTS = 176
 NEAR_FIRST = (1, 3, 2)
 
 
@@ -125,6 +125,7 @@
     t = lax.axis_index("tm")
     q = lax.axis_index("patch")
     y, g = t // 4, t % 4
+    part_at = lax.axis_index("dp")
     x, c = q // 2, q % 2
     copies = Copies(send_sem, recv_sem)
 
@@ -148,6 +149,9 @@
 
     def to_patch(d):
         return {"patch": (q + d) % 8}
+
+    def to_dp(m):
+        return {"dp": (part_at + m) % 4}
 
     sibling = {"patch": x * 2 + 1 - c}
     after = {"tm": (t + 1) % 16}
@@ -181,6 +185,7 @@
         + [to_y(d) for d in (1, 2, 3)]
         + [to_patch(d) for d in range(1, 8)]
         + [after, before]
+        + [to_dp(m) for m in (1, 2, 3)]
     )
     for partner in partners:
         pl.semaphore_signal(barrier, inc=1, device_id=partner, device_id_type=MESH)
@@ -200,10 +205,31 @@
 
     pl.semaphore_wait(barrier, len(partners))
 
-    for d in NEAR_FIRST:
-        copies.send(f"wqkv_z{d}", wqkv.at[q, 0], wqkv.at[q, d], to_z(d))
-    for d in NEAR_FIRST:
-        copies.send(f"wout_z{d}", wout.at[q, 0, 0], wout.at[q, 0, d], to_z(d))
+    def qkv_quarter(d, of):
+        return wqkv.at[q, d, pl.ds(pl.multiple_of(of * 48, 16), 48)]
+
+    def out_quarter(d, of):
+        return wout.at[q, 0, d, pl.ds(pl.multiple_of(of * 16, 16), 16)]
+
+    def quarter_z(name, quarter):
+        for d in NEAR_FIRST:
+            copies.send((name, "z", d), quarter(0, part_at), quarter(d, part_at), to_z(d))
+
+    def quarter_dp(name, quarter):
+        for d in NEAR_FIRST:
+            copies.wait((name, "z", d), quarter(d, part_at), to_z(d))
+            for m in (1, 3, 2):
+                copies.send(
+                    (name, "dp", d, m), quarter(d, part_at), quarter(d, part_at), to_dp(m)
+                )
+
+    def quarter_end(name, quarter):
+        for d in NEAR_FIRST:
+            for m in (1, 3, 2):
+                copies.wait((name, "dp", d, m), quarter(d, (part_at + 4 - m) % 4), to_dp(m))
+
+    quarter_z("wqkv", qkv_quarter)
+    quarter_z("wout", out_quarter)
     def send_rows(position):
         for d in NEAR_FIRST:
             copies.send(
@@ -247,6 +273,7 @@
     for position in range(2):
         rows[position, g] = own_rows[position, g]
         spread_rows(position, 0, g)
+    quarter_dp("wqkv", qkv_quarter)
 
     latn[...] = layer_norm(latents_ref[...].astype(F32), latent_gain_ref[...]).astype(BF16)
     queries = dot_nt(query_w_ref[...], latn[...])
@@ -292,11 +319,10 @@
         lambda buf, at: buf.at[at, pl.ds(2, 2)],
     )
 
-    for d in NEAR_FIRST:
-        copies.wait(f"wqkv_z{d}", wqkv.at[q, d], to_z(d))
+    quarter_dp("wout", out_quarter)
+    quarter_end("wqkv", qkv_quarter)
     unit_start(*qkv_unit[:3])
-    for d in NEAR_FIRST:
-        copies.wait(f"wout_z{d}", wout.at[q, 0, d], to_z(d))
+    quarter_end("wout", out_quarter)
     for d in NEAR_FIRST:
         copies.send(f"wout_y{d}", wout.at[q, 0], wout.at[q, d], to_y(d))
     receive_rows(0)

time: 104 us -> 104 us (level)
  the two profiles are of different devices: /device:TPU:45 before, /device:TPU:1 now
where the time goes in v5:
time: 104 us
  Pallas kernels  100 us (96%)
  local copies, waits for them, and re-layouts  2.42 us (2%)
  between operations  1.3 us (1%)
    pallas_call x1, Pallas kernels, on_device(): pl.pallas_call(kernel, out_shape=(jax.ShapeDtypeStruct((128, D), BF16), j...  100 us
    unnamed x4, local copies, waits for them, and re-layouts  2.42 us

profile of v5, /device:TPU:1, one launch (start us, length us, event | category | flops | bytes accessed | tf_op | source)
XLA Modules:
  0.0 103.9 jit_solution(12660019072817749846)
XLA Ops:
  1.3 100.2 %shard_map.122 = (bf16[128,1024]{1,0:T(8,128)(2,1)}, bf16[128,1024]{1,0:T(8,128)(2,1)}) custom-call(s32[2]{0:T(128)} %starts_hbm.1, s32[1]{0:T(128)S(6)} %copy.15.valid_hbm, bf16[128,1024]{1,0:T(8,128)(2,1)} %bitcast.11, f32[1,1024]{1,0:T(1,128)} %bitcast.13, bf16[192,1024]{1,0:T(8,128)(2,1)} %bitcast.8, bf16[64,1024]{1,0:T(8,128)(2,1)} %out_w_hbm.1, ...), custom_call_target="tpu_custom_call" | custom-call | tf_op jit(solution)/shard_map/pallas_call | solution.py:617
  101.5 0.0 copy-start
  101.5 1.7 %copy.16 = bf16[16,8,1024]{2,1,0:T(8,128)(2,1)} copy(bf16[16,8,1024]{2,1,0:T(8,128)(2,1)} %bitcast.10) | data formatting | bytes 524288
  103.2 0.0 copy-done
  103.2 0.7 copy.17
Async XLA Ops:
  101.5 1.7 %copy-start = (bf16[128,1024]{1,0:T(8,128)(2,1)S(1)}, bf16[128,1024]{1,0:T(8,128)(2,1)}, u32[]{:S(2)}) copy-start(bf16[128,1024]{1,0:T(8,128)(2,1)} %get-tuple-element.5) | copy-start | bytes 786436
